TPU v7x, 256 devices: a whole 4x4x8 slice. The times are simulated.
256 devices in a mesh: slab: 8 (over x_hi, y), cell: 32 (over z, x_lo, core).
Axes of the slice: x: 4 (x_hi: 2, x_lo: 2; x = x_hi * 2 + x_lo), y: 4, z: 8, core: 2. Of those that a mesh axis runs over, the one named last changes fastest.
Arguments:
- positions: float32 [3, 2097152], P(None, ('slab', 'cell')), may hold values from 0 to 32, as said below
- burgers: float32 [3, 2097152], P(None, ('slab', 'cell')), may hold values from -0.018 to 0.018
- mobility: float32 [2097152], P(('slab', 'cell')), may hold values from 0.5 to 2
- near_list: int32 [16384, 6], P(('slab', 'cell')), may hold values from 0 to 255
- near_count: int32 [16384], P(('slab', 'cell')), may hold values from 1 to 6, as said below
- send_list: int32 [4, 12288], P(None, ('slab', 'cell')), may hold values from 0 to 63
Outputs:
- displacement: float32 [3, 2097152], P(None, ('slab', 'cell'))
- velocity: float32 [3, 2097152], P(None, ('slab', 'cell'))
Inputs may be any that keep to these rules, and one draw needn't show every extreme that they name: `positions`: cell (s, c) owns the segments of its block of 8192; every coordinate lies in that cell's box. `near_count`: some cells carry pile-ups with up to 6 live slots a block; the others have 1 or 2.
All inputs are finite; a program needn't handle non-finite values.
Results may differ from a plain program's by a relative error of at most 0.00035.
Values sent between devices are 32-bit elements; how exact they have to be, the bound alone decides.
No kernel may reach another device: no remote copies, remote signals or barrier semaphores. Data moves between devices by JAX's collectives and lax.ppermute only.
A program may use at most 128 MiB of HBM per device.

v0:
```python
import functools

import jax
import jax.numpy as jnp
from jax import lax
from jax.experimental import pallas as pl
from jax.experimental.pallas import tpu as pltpu
from jax.sharding import PartitionSpec as P

SUBSTEPS = 4
BLOCKS = 64
LANES = 128
NEAR = 6
GHOST = 48
EXT = 256
GROUP = 8
LEAD = GROUP
TAIL = 56
AT_SENDS = 8
AT_PAIRS = AT_SENDS + 4 * GHOST + LEAD
LIST = BLOCKS * NEAR + TAIL + LEAD
CONTROL = AT_PAIRS + 2 * LIST + 8
EARLY, LATE = (3,), (0, 2, 1)
SHARE = 9

core_sq = 0.04
far_sq = 1.0
time_step = 0.2

f32 = jnp.float32
bf16 = jnp.bfloat16

vmem = pl.BlockSpec(memory_space=pltpu.VMEM)
smem = pl.BlockSpec(memory_space=pltpu.SMEM)
params = pltpu.CompilerParams(vmem_limit_bytes=40 * 2**20)


def round_bf16(x):
    return x.astype(bf16).astype(f32)


def split2(x):
    high = x.astype(bf16)
    return high, (x - high.astype(f32)).astype(bf16)


def split3(x):
    high = round_bf16(x)
    rest = x - high
    mid = round_bf16(rest)
    return high, mid, round_bf16(rest - mid)


def parity():
    return lax.axis_index("slab") % 2, lax.axis_index("cell") % 2


def send_rows():
    odd_slab, odd_cell = parity()
    return odd_slab, 1 - odd_slab, 3 - odd_cell, 2 + odd_cell


def slot_moves():
    odd_slab, odd_cell = parity()
    return (
        GHOST * (1 - odd_slab),
        GHOST * (odd_slab - 1),
        GHOST * odd_cell,
        -GHOST * odd_cell,
    )


def slot_shifts():
    odd_slab, odd_cell = parity()
    along_slab = (1 - 2 * odd_slab).astype(f32)
    along_cell = (1 - 2 * odd_cell).astype(f32)
    return (0, along_slab), (0, -along_slab), (1, -along_cell), (1, along_cell)


def slot_exists():
    out = []
    for axis in ("slab", "cell"):
        i = lax.axis_index(axis)
        partner = i - 1 + 2 * (i % 2)
        out.append((partner >= 0) & (partner < lax.axis_size(axis)))
    return None, out[0], out[1], None


def fill_sends(block_of, sources, sends):
    def body(n, carry):
        for d in sends:
            block = block_of(d, n)
            for a, (ref, index) in enumerate(sources):
                sends[d][a, pl.ds(n, 1), :] = ref[index, pl.ds(block, 1), :]
        return carry

    lax.fori_loop(0, GHOST, body, 0, unroll=4)


def send_now(control, now, sends):
    fill_sends(
        lambda d, n: control[AT_SENDS + GHOST * d + n],
        [(now, k) for k in range(3)],
        dict(enumerate(sends)),
    )


def centre_of():
    slab = lax.axis_index("slab").astype(f32)
    cell = lax.axis_index("cell").astype(f32)
    return slab, cell


def list_pairs(near_list, near_count):
    segment = (near_list + (GHOST - BLOCKS)) // GHOST
    exists = {0: None, 3: None}
    exists[1], exists[2] = slot_exists()[1:3]
    odd_slab, odd_cell = parity()
    sides = (
        (odd_slab == 1) | exists[1],
        (odd_slab == 0) | exists[1],
        (odd_cell == 1) | exists[2],
        (odd_cell == 0) | exists[2],
    )
    slot = lax.broadcasted_iota(jnp.int32, near_list.shape, 0)
    block = lax.broadcasted_iota(jnp.int32, near_list.shape, 1)
    live = jnp.where(slot < near_count, 1, 0)
    moved = near_list
    for i, (move, there) in enumerate(zip(slot_moves(), sides)):
        mine = segment == 1 + i
        moved = moved + jnp.where(mine, move, 0)
        live = jnp.where(mine, live * there.astype(jnp.int32), live)
    late = jnp.where(moved >= BLOCKS, live, 0)
    for d in EARLY:
        first = BLOCKS + GHOST * d
        late = jnp.where((moved >= first) & (moved < first + GHOST), 0, late)
    earlier = lax.broadcasted_iota(jnp.int32, (BLOCKS, BLOCKS), 0) < lax.broadcasted_iota(
        jnp.int32, (BLOCKS, BLOCKS), 1
    )
    place = jnp.full(near_list.shape, 2 * LIST, jnp.int32)
    amounts = []
    for i, mine in enumerate((live - late, late)):
        rows = [mine[n : n + 1] for n in range(NEAR)]
        before = [jnp.zeros_like(rows[0])]
        for row in rows:
            before.append(before[-1] + row)
        amount = before.pop().astype(f32)
        offset = jnp.dot(
            jnp.broadcast_to(amount, (8, BLOCKS)),
            jnp.where(earlier, 1.0, 0.0),
            preferred_element_type=f32,
        )[:1]
        at = jnp.concatenate([offset.astype(jnp.int32) + x for x in before], axis=0)
        place = jnp.where(mine > 0, at + LIST * i, place)
        amounts.append(jnp.sum(amount, axis=1, keepdims=True).astype(jnp.int32))
    words = 2**15 * place + 2**SHARE * block + moved
    return words, amounts


def pack_kernel(numbers_smem, numbers, positions, burgers, places, scalars, s3, s0, s2, s1):
    slab, cell = centre_of()
    for k, by in enumerate((slab + 0.5, cell + 0.5, 0.5)):
        places[k] = positions[k] - by
    scalars[...] = jnp.zeros_like(scalars)
    words, amounts = list_pairs(numbers[:NEAR, :BLOCKS], numbers[NEAR : NEAR + 1, :BLOCKS])
    scalars[:NEAR, :BLOCKS] = words
    for i in range(2):
        scalars[NEAR + i : NEAR + i + 1, :] = jnp.broadcast_to(amounts[i], (1, LANES))
    rows = send_rows()
    for d in range(4):
        first = 2 * (d // 2)
        scalars[8 + d : 9 + d, :] = jnp.where(
            rows[d] == first, numbers[8 + first : 9 + first, :], numbers[9 + first : 10 + first, :]
        )
    sources = [(places, k) for k in range(3)] + [(burgers, a) for a in range(3)]
    fill_sends(lambda d, n: numbers_smem[8 + rows[d], n], sources, {0: s0, 1: s1, 2: s2, 3: s3})


def put_rows(out, k, value):
    for b in range(BLOCKS):
        out[k : k + 1, LANES * b : LANES * b + LANES] = value[b : b + 1]


def halves(tile):
    low = lax.broadcasted_iota(jnp.int32, (8, LANES), 0) < 4
    turned = pltpu.roll(tile, 4, 0)
    return jnp.where(low, tile, turned), jnp.where(low, turned, tile)


def pair_rows(values):
    low = lax.broadcasted_iota(jnp.int32, (8, LANES), 0) < 4
    rows = [
        x if x is y else jnp.where(low, x, y) for x, y in zip(values[0::2], values[1::2])
    ]
    rows += [jnp.zeros((8, LANES), f32)] * (LANES // 8 - len(rows))
    return jnp.concatenate(rows, axis=0)


def far_kernel(
    scalars, places, burgers, out, control, acc, rows, cols, apart_by, w_even, w_odd
):
    amounts = [scalars[NEAR, 0], scalars[NEAR + 1, 0]]
    for i in range(LEAD):
        control[AT_PAIRS - LEAD + i] = EXT
        control[AT_PAIRS + LIST - LEAD + i] = EXT
    for tile in range(BLOCKS // 8):
        p = [halves(places[k, 8 * tile : 8 * tile + 8, :]) for k in range(3)]
        burg = [halves(burgers[a, 8 * tile : 8 * tile + 8, :]) for a in range(3)]
        for half in range(2):
            here = [x[half] for x in p]
            sources = [x[half] for x in burg]
            moments = [x * y for x in here for y in sources]
            values = []
            for group in (sources, moments):
                high = [round_bf16(x) for x in group]
                values += high + [x - h for x, h in zip(group, high)]
            rows[2 * tile + half] = pair_rows(values)
            one = jnp.ones((8, LANES), f32)
            square = sum(x * x for x in here) + far_sq
            values = [part for x in (here[0], here[1], square) for part in split3(x)]
            cols[2 * tile + half] = pair_rows(values + [one, one, one]).T.astype(bf16)
    acc[...] = jnp.zeros_like(acc)
    w_odd[...] = jnp.zeros_like(w_odd)
    slab, cell = centre_of()
    target = lax.broadcasted_iota(jnp.int32, (1, EXT), 1)
    apart = [(target // 32).astype(f32) - slab, (target % 32).astype(f32) - cell]
    square = apart[0] * apart[0] + apart[1] * apart[1]
    square_high = round_bf16(square)
    place = lax.broadcasted_iota(jnp.int32, (LANES, EXT), 0)
    values = jnp.where(place < 36, 1.0, 0.0)
    for first, last, x in (
        (0, 12, -2.0 * apart[0]),
        (12, 24, -2.0 * apart[1]),
        (36, 40, square_high),
        (40, 44, square - square_high),
    ):
        values = jnp.where((place >= first) & (place < last), x, values)
    for g in range(4):
        apart_by[g] = jnp.where(place % 4 == g, values, 0.0).astype(bf16)

    def sums(group, g, w):
        mine = rows[group, pl.ds(g, 32, stride=4), :].astype(bf16)
        acc[...] += jnp.dot(
            jnp.concatenate([mine, mine], axis=1), w[g], preferred_element_type=f32
        )

    def half(group, w_now, w_before):
        for i in range(4):
            for slot in range(NEAR):
                word = scalars[slot, 4 * group + i]
                at = lax.shift_right_logical(word, 15)
                control[AT_PAIRS + at] = word & (2**15 - 1)
        for d in range(4):
            for i in range(3):
                n = 3 * group + i
                control[AT_SENDS + GHOST * d + n] = scalars[8 + d, n]
        for g in range(4):
            sums(jnp.maximum(group - 1, 0), g, w_before)
            r = lax.rsqrt(jnp.dot(cols[group], apart_by[g], preferred_element_type=f32))
            r2 = r * r
            w3 = r2 * r
            for k, w in enumerate((w3, w3 * r2)):
                high, low = split2(w)
                w_now[g, :LANES, EXT * k : EXT * k + EXT] = high
                w_now[g, LANES:, EXT * k : EXT * k + EXT] = low

    def body(step, carry):
        half(2 * step, w_even, w_odd)
        half(2 * step + 1, w_odd, w_even)
        return carry

    lax.fori_loop(0, BLOCKS // 8, body, 0)
    for g in range(4):
        sums(BLOCKS // 4 - 1, g, w_odd)
    for k in range(2):
        for i in range(TAIL):
            control[AT_PAIRS + LIST * k + amounts[k] + i] = EXT
        control[k] = amounts[k]

    apart = apart + [jnp.zeros((1, EXT), f32)]

    def row(k, i):
        return acc[i : i + 1, EXT * k : EXT * k + EXT]

    direct = [row(0, a) + row(0, 3 + a) for a in range(3)]
    total = [row(1, a) + row(1, 3 + a) for a in range(3)]
    gradient = []
    for a in range(3):
        for k in range(3):
            moment = row(1, 6 + 3 * k + a) + row(1, 15 + 3 * k + a)
            gradient.append(-3.0 * (apart[k] * total[a] - moment))
    zero = jnp.zeros((LANES - 12, 2 * LANES), f32)
    values = jnp.concatenate(direct + gradient + [zero], axis=0)
    out[...] = jnp.concatenate([values[:, :LANES].T, values[:, LANES:].T], axis=0)


def tile_of(own, ghosts, index, tile):
    if tile < BLOCKS // 8:
        return own[index, 8 * tile : 8 * tile + 8, :]
    d, n = divmod(tile - BLOCKS // 8, GHOST // 8)
    return ghosts[d][index, 8 * n : 8 * n + 8, :]


def tiles_of(slots):
    n = GHOST // 8
    return [BLOCKS // 8 + n * d + i for d in slots for i in range(n)]


def prepare_sources(own, ghosts, tiles, left):
    shift = slot_shifts()
    one = jnp.ones((8, LANES), f32)
    low = lax.broadcasted_iota(jnp.int32, (8, LANES), 0) < 4

    for tile in tiles:
        p = [tile_of(own, ghosts, k, tile) for k in range(3)]
        if tile >= BLOCKS // 8:
            k, by = shift[(tile - BLOCKS // 8) // (GHOST // 8)]
            p[k] = p[k] + by
        parts_of = [split3(x) for x in p]
        parts_of.append(split3(p[0] * p[0] + p[1] * p[1] + p[2] * p[2]))
        turned = [[pltpu.roll(x, 4, 0) for x in group] for group in parts_of]
        for half in range(2):
            first, second = (parts_of, turned) if half == 0 else (turned, parts_of)
            values = []
            for (h, m, _), (h2, m2, l2) in zip(first[:3], second[:3]):
                values += [
                    jnp.where(low, h, h2),
                    jnp.where(low, m, m2),
                    jnp.where(low, h, l2),
                ]
            h, _, l = first[3]
            values += [jnp.where(low, h, second[3][1]), jnp.where(low, l, one), one]
            values += [jnp.zeros((8, LANES), f32)] * (LANES // 8 - len(values))
            left[2 * tile + half] = jnp.concatenate(values, axis=0).T.astype(bf16)
    left[EXT // 4] = jnp.zeros((LANES, LANES), bf16)


def prepare_targets(own, parts, right):
    one = jnp.ones((8, LANES), f32)
    low = lax.broadcasted_iota(jnp.int32, (8, LANES), 0) < 4

    x = [own[k] for k in range(3)]
    for k in range(3):
        for i, part in enumerate(split3(-2.0 * x[k])):
            parts[3 * k + i] = part
    for i, part in enumerate(split3(x[0] * x[0] + x[1] * x[1] + x[2] * x[2] + core_sq)):
        parts[9 + i] = part
    for b in range(BLOCKS):
        def row(i):
            return jnp.broadcast_to(parts[i, b : b + 1, :], (8, LANES))

        rows = []
        for k in range(3):
            h, m, l = row(3 * k), row(3 * k + 1), row(3 * k + 2)
            high_mid = jnp.where(low, h, m)
            rows += [high_mid, high_mid, jnp.where(low, l, h)]
        rows += [one, jnp.where(low, one, row(9)), jnp.where(low, row(10), row(11))]
        for i in range(6):
            right[b, i] = jnp.concatenate(rows[2 * i : 2 * i + 2], axis=0).astype(bf16)
        right[b, 6:] = jnp.zeros((2, 16, LANES), bf16)


def add_pairs(control, which, burg, left, right, mask, acc, k_even, k_odd):
    place = lax.broadcasted_iota(jnp.int32, (16, LANES), 0) % 4
    for g in range(4):
        mask[g] = jnp.where(place == g, 1.0, 0.0).astype(bf16)

    k_odd[...] = jnp.zeros_like(k_odd)

    def pair(i):
        word = control[AT_PAIRS + LIST * which + i]
        return lax.shift_right_logical(word, SHARE), word & (2**SHARE - 1)

    def sums(step, g, k_before):
        i = step * GROUP + g
        (b0, t0), (b1, t1) = pair(i), pair(i + 1)
        rows = jnp.concatenate(
            [burg[pl.ds(pl.multiple_of(8 * t, 8), 8), :] for t in (t0, t1)], axis=0
        ).astype(bf16)
        both = jnp.dot(
            jnp.concatenate([rows, rows], axis=1),
            jnp.concatenate([k_before[g], k_before[g + 1]], axis=1),
            preferred_element_type=f32,
        )
        at = pl.ds(pl.multiple_of(8 * b0, 8), 8)
        acc[at, :] = acc[at, :] + both[:8, :LANES]
        at = pl.ds(pl.multiple_of(8 * b1, 8), 8)
        acc[at, :] = acc[at, :] + both[8:, LANES:]

    def half(step, k_now, k_before):
        for g in range(GROUP):
            if g % 2 == 0:
                sums(step - 1, g, k_before)
            b, t = pair(step * GROUP + g)
            features = (right[b] * mask[t & 3][None]).reshape(LANES, LANES)
            near_sq = jnp.dot(
                left[lax.shift_right_logical(t, 2)], features, preferred_element_type=f32
            )
            near_sq = jnp.maximum(near_sq, core_sq)
            r = lax.rsqrt(near_sq)
            q = lax.rsqrt(near_sq + (far_sq - core_sq))
            high, low = split2(r * r * r - q * q * q)
            k_now[g, :LANES, :] = high
            k_now[g, LANES:, :] = low

    def body(step, carry):
        half(2 * step, k_even, k_odd)
        half(2 * step + 1, k_odd, k_even)
        return carry

    steps = (control[which] + 2 * GROUP - 1) // (2 * GROUP)
    lax.fori_loop(0, steps, body, 0)
    for g in range(0, GROUP, 2):
        sums(2 * steps - 1, g, k_odd)


def component(acc, a):
    return acc[pl.ds(a, BLOCKS, stride=8), :] + acc[pl.ds(3 + a, BLOCKS, stride=8), :]


parts_scratch = pltpu.VMEM((12, BLOCKS, LANES), f32)
right_shape = (BLOCKS, 8, 16, LANES)
acc_shape = (BLOCKS * 8, LANES)
near_scratch = [
    pltpu.VMEM((EXT // 4 + 1, LANES, LANES), bf16),
    pltpu.VMEM((4, 16, LANES), bf16),
    pltpu.VMEM((GROUP, 2 * LANES, LANES), bf16),
    pltpu.VMEM((GROUP, 2 * LANES, LANES), bf16),
]


def total_force(expansion, near, places):
    out = []
    for a in range(3):
        far = expansion[0:1, a : a + 1]
        for k in range(3):
            far = far + expansion[0:1, 3 + 3 * a + k : 4 + 3 * a + k] * places[k]
        out.append(near[a] + far)
    return out


def first_kernel(
    control, own, burgers, g3, g0, g2, g1, near, burg, left, mask, k_even, k_odd, parts, right, acc
):
    ghosts = (g0, g1, g2, g3)
    exists = slot_exists()
    burg[...] = jnp.zeros_like(burg)
    for tile in range(EXT // 8):
        for a in range(3):
            if tile < BLOCKS // 8:
                value = burgers[a, 8 * tile : 8 * tile + 8, :]
            else:
                d = (tile - BLOCKS // 8) // (GHOST // 8)
                value = tile_of(None, ghosts, 3 + a, tile)
                if exists[d] is not None:
                    value = jnp.where(exists[d], value, 0.0)
            high = round_bf16(value)
            burg[pl.ds(tile * 64 + a, 8, stride=8), :] = high
            burg[pl.ds(tile * 64 + 3 + a, 8, stride=8), :] = value - high
    prepare_sources(own, ghosts, range(EXT // 8), left)
    prepare_targets(own, parts, right)
    acc[...] = jnp.zeros_like(acc)
    for which in range(2):
        add_pairs(control, which, burg, left, right, mask, acc, k_even, k_odd)
    for a in range(3):
        near[a] = component(acc, a)


def start_kernel(control, shares, near, places, mobility, expansion, moved, now, *sends):
    expansion[...] = jnp.broadcast_to(jnp.sum(shares[...], axis=0, keepdims=True), (8, LANES))
    p = [places[k] for k in range(3)]
    force = total_force(expansion[...], [near[a] for a in range(3)], p)
    for a in range(3):
        step = (time_step * mobility[...]) * force[a]
        moved[a] = step
        now[a] = p[a] + step
    send_now(control, now, sends)


def early_kernel(control, own, g3, burg, right, acc, left, mask, k_even, k_odd, parts):
    ghosts = (None, None, None, g3)
    prepare_sources(own, ghosts, list(range(BLOCKS // 8)) + tiles_of(EARLY), left)
    prepare_targets(own, parts, right)
    acc[...] = jnp.zeros_like(acc)
    add_pairs(control, 0, burg, left, right, mask, acc, k_even, k_odd)


def late_force(control, expansion, own, g0, g2, g1, burg, right, acc_in, left, mask, k_even, k_odd, acc):
    prepare_sources(own, (g0, g1, g2, None), tiles_of(LATE), left)
    acc[...] = acc_in[...]
    add_pairs(control, 1, burg, left, right, mask, acc, k_even, k_odd)
    return total_force(
        expansion[...], [component(acc, a) for a in range(3)], [own[k] for k in range(3)]
    )


def step_kernel(
    final, control, expansion, own, g0, g2, g1, burg, right, acc_in, mobility, places, moved,
    new_moved, now, s0, s1, s2, s3, *scratch
):
    force = late_force(control, expansion, own, g0, g2, g1, burg, right, acc_in, *scratch)
    for a in range(3):
        total = moved[a] + (time_step * mobility[...]) * force[a]
        if final:
            put_rows(new_moved, a, total)
        else:
            new_moved[a] = total
        now[a] = places[a] + total
    send_now(control, now, (s0, s1, s2, s3))


def last_kernel(
    control, expansion, own, g0, g2, g1, burg, right, acc_in, mobility, velocity, *scratch
):
    force = late_force(control, expansion, own, g0, g2, g1, burg, right, acc_in, *scratch)
    for a in range(3):
        put_rows(velocity, a, mobility[...] * force[a])


def cost(flops):
    return pl.CostEstimate(flops=int(flops), bytes_accessed=2**20, transcendentals=0)


def shape(*dims, dtype=f32):
    return jax.ShapeDtypeStruct(dims, dtype)


def swap(x, slot):
    n_slabs, n_cells = lax.axis_size("slab"), lax.axis_size("cell")
    pairs = []
    for s in range(n_slabs):
        for c in range(n_cells):
            if slot == 0:
                to = (s ^ 1, c)
            elif slot == 3:
                to = (s, c ^ 1)
            elif slot == 1:
                t = s - 1 + 2 * (s % 2)
                to = (t, c) if 0 <= t < n_slabs else (s, c ^ 1)
            else:
                t = c - 1 + 2 * (c % 2)
                to = (s, t) if 0 <= t < n_cells else (s ^ 1, c)
            pairs.append((s * n_cells + c, to[0] * n_cells + to[1]))
    return lax.ppermute(x, ("slab", "cell"), pairs)


def exchange(sends):
    return [swap(sends[slot], slot) for slot in EARLY + LATE]


def local(positions, burgers, mobility, near_list, near_count, send_list):
    mobility = mobility.reshape(BLOCKS, LANES)
    flat = shape(*positions.shape)
    block = shape(3, BLOCKS, LANES)
    send = shape(3, GHOST, LANES)

    positions = positions.reshape(block.shape)
    burgers = burgers.reshape(block.shape)
    numbers = (
        jnp.pad(near_list.T, ((0, 16 - NEAR), (0, LANES - BLOCKS)))
        + jnp.pad(near_count[None], ((NEAR, 15 - NEAR), (0, LANES - BLOCKS)))
        + jnp.pad(send_list, ((8, 4), (0, LANES - GHOST)))
    )

    places, scalars, *sends = pl.pallas_call(
        pack_kernel,
        out_shape=[block, shape(16, LANES, dtype=jnp.int32)] + [shape(6, GHOST, LANES)] * 4,
        in_specs=[smem, vmem, vmem, vmem],
        out_specs=[vmem] * 6,
        compiler_params=params,
        name="pack",
    )(numbers, numbers, positions, burgers)
    ghosts = [swap(x, slot) for x, slot in zip(sends, (3, 0, 2, 1))]

    shares, control = pl.pallas_call(
        far_kernel,
        out_shape=[shape(EXT, LANES), shape(CONTROL, dtype=jnp.int32)],
        in_specs=[smem, vmem, vmem],
        out_specs=[vmem, smem],
        scratch_shapes=[
            pltpu.VMEM((32, 2 * EXT), f32),
            pltpu.VMEM((BLOCKS // 4, LANES, LANES), f32),
            pltpu.VMEM((BLOCKS // 4, LANES, LANES), bf16),
            pltpu.VMEM((4, LANES, EXT), bf16),
            pltpu.VMEM((4, 2 * LANES, 2 * EXT), bf16),
            pltpu.VMEM((4, 2 * LANES, 2 * EXT), bf16),
        ],
        compiler_params=params,
        cost_estimate=cost(20e9),
        name="far",
    )(scalars, places, burgers)
    shares = lax.all_to_all(shares, ("slab", "cell"), 0, 0, tiled=True)

    near, burg = pl.pallas_call(
        first_kernel,
        out_shape=[block, shape((EXT + 1) * 8, LANES)],
        in_specs=[smem] + [vmem] * 6,
        out_specs=[vmem] * 2,
        scratch_shapes=near_scratch
        + [parts_scratch, pltpu.VMEM(right_shape, bf16), pltpu.VMEM(acc_shape, f32)],
        compiler_params=params,
        cost_estimate=cost(20e9),
        name="near_first",
    )(control, places, burgers, *ghosts)

    expansion, moved, now, *sends = pl.pallas_call(
        start_kernel,
        out_shape=[shape(8, LANES), block, block] + [send] * 4,
        in_specs=[smem] + [vmem] * 4,
        out_specs=[vmem] * 7,
        compiler_params=params,
        name="start",
    )(control, shares, near, places, mobility)

    def evaluate(kernel, out_shape, name, *more):
        ghosts = exchange(sends)
        right, acc = pl.pallas_call(
            early_kernel,
            out_shape=[shape(*right_shape, dtype=bf16), shape(*acc_shape)],
            in_specs=[smem] + [vmem] * 3,
            out_specs=[vmem] * 2,
            scratch_shapes=near_scratch + [parts_scratch],
            compiler_params=params,
            cost_estimate=cost(20e9),
            name="near_early",
        )(control, now, *ghosts[: len(EARLY)], burg)
        return pl.pallas_call(
            kernel,
            out_shape=out_shape,
            in_specs=[smem] + [vmem] * (6 + len(LATE) + len(more)),
            out_specs=jax.tree.map(lambda _: vmem, out_shape),
            scratch_shapes=near_scratch + [pltpu.VMEM(acc_shape, f32)],
            compiler_params=params,
            cost_estimate=cost(10e9),
            name=name,
        )(control, expansion, now, *ghosts[len(EARLY) :], burg, right, acc, mobility, *more)

    for substep in range(1, SUBSTEPS):
        final = substep == SUBSTEPS - 1
        moved, now, *sends = evaluate(
            functools.partial(step_kernel, final),
            [flat if final else block, block] + [send] * 4,
            "near_step",
            places,
            moved,
        )
    velocity = evaluate(last_kernel, flat, "near_last")
    return moved, velocity


def solution(mesh):
    return jax.shard_map(
        local,
        mesh=mesh,
        in_specs=(
            P(None, ("slab", "cell")),
            P(None, ("slab", "cell")),
            P(("slab", "cell")),
            P(("slab", "cell"), None),
            P(("slab", "cell")),
            P(None, ("slab", "cell")),
        ),
        out_specs=(P(None, ("slab", "cell")), P(None, ("slab", "cell"))),
        check_vma=False,
    )
```

profile of v0, /device:TPU:103, one launch (start us, length us, event | category | flops | bytes accessed | tf_op | source)
XLA Modules:
  0.0 113.2 jit_solution(4915611895567630626)
XLA Ops:
  0.6 1.0 copy_bitcast_fusion
  2.3 1.5 %pack.1 = (f32[3,64,128]{2,1,0:T(8,128)S(1)}, s32[16,128]{1,0:T(8,128)S(1)}, f32[6,48,128]{2,1,0:T(8,128)S(1)}, f32[6,48,128]{2,1,0:T(8,128)S(1)}, f32[6,48,128]{2,1,0:T(8,128)S(1)}, /*index=5*/f32[6,48,128]{2,1,0:T(8,128)S(1)}) custom-call(s32[16,128]{1,0:T(8,128)S(1)} %pad_add_fusion.numbers_smem.numbers, s32[16,128]{1,0:T(8,128)S(1)} %pad_add_fusion.numbers_smem.numbers, ...), custom_call_target="tpu_custom_call" | custom-call | tf_op jit(solution)/shard_map/pack/pallas_call | solution.py:565
  3.9 0.8 collective-permute-start
  4.6 1.3 %collective-permute-start.1 = (f32[6,48,128]{2,1,0:T(8,128)S(1)}, f32[6,48,128]{2,1,0:T(8,128)S(1)}, u32[]{:S(2)}, u32[]{:S(2)}) collective-permute-start(f32[6,48,128]{2,1,0:T(8,128)S(1)} %get-tuple-element.50), channel_id=1, source_target_pairs={{0,32},{1,33},{2,34},{3,35},{4,36},{5,37},{6,38},{7,39},{8,40},{9,... | collective-permute-start | bytes 442376 | tf_op jit(solution)/shard_map/ppermute | solution.py:544
  5.9 3.4 %collective-permute-start.2 = (f32[6,48,128]{2,1,0:T(8,128)S(1)}, f32[6,48,128]{2,1,0:T(8,128)S(1)}, u32[]{:S(2)}, u32[]{:S(2)}) collective-permute-start(f32[6,48,128]{2,1,0:T(8,128)S(1)} %get-tuple-element.51), channel_id=1, source_target_pairs={{0,32},{1,2},{2,1},{3,4},{4,3},{5,6},{6,5},{7,8},{8,7},{9,10},{10,... | collective-permute-start | bytes 442376 | tf_op jit(solution)/shard_map/ppermute | solution.py:544
  9.3 2.4 %collective-permute-start.3 = (f32[6,48,128]{2,1,0:T(8,128)S(1)}, f32[6,48,128]{2,1,0:T(8,128)S(1)}, u32[]{:S(2)}, u32[]{:S(2)}) collective-permute-start(f32[6,48,128]{2,1,0:T(8,128)S(1)} %get-tuple-element.52), channel_id=1, source_target_pairs={{0,1},{1,0},{2,3},{3,2},{4,5},{5,4},{6,7},{7,6},{8,9},{9,8},{10,11... | collective-permute-start | bytes 442376 | tf_op jit(solution)/shard_map/ppermute | solution.py:544
  11.7 7.3 %far.1 = (f32[256,128]{1,0:T(8,128)}, s32[1112]{0:T(1024)S(1)}) custom-call(s32[16,128]{1,0:T(8,128)S(1)} %get-tuple-element.45.scalars, f32[3,64,128]{2,1,0:T(8,128)S(1)} %get-tuple-element.46.places.own, f32[3,64,128]{2,1,0:T(8,128)S(1)} %get-tuple-element.88.burgers), custom_call_target="tpu_custom_call" | custom-call | flops 20000000000 | bytes 1048576 | tf_op jit(solution)/shard_map/far/pallas_call | solution.py:575
  19.1 9.2 %all-to-all-start = ((f32[256,1,128]{2,1,0:T(1,128)}), f32[256,1,128]{2,1,0:T(1,128)S(1)}, u32[]{:S(2)}, u32[]{:S(2)}) async-start(f32[256,1,128]{2,1,0:T(1,128)} %bitcast.3), calls=%async_computation | async-start | bytes 262144 | tf_op jit(solution)/shard_map/all_to_all | solution.py:592
  28.3 12.0 %near_first.1 = (f32[3,64,128]{2,1,0:T(8,128)S(1)}, f32[2056,128]{1,0:T(8,128)S(1)}) custom-call(s32[1112]{0:T(1024)S(1)} %get-tuple-element.47.control, f32[3,64,128]{2,1,0:T(8,128)S(1)} %get-tuple-element.46.places.own, f32[3,64,128]{2,1,0:T(8,128)S(1)} %get-tuple-element.88.burgers, f32[6,48,128]{2,1,0:T(8,128)S(1)} %collective-permute-done.g3, ...), custom_call_target="tpu_custom_call" | custom-call | flops 20000000000 | bytes 1048576 | tf_op jit(solution)/shard_map/near_first/pallas_call | solution.py:594
  40.4 1.1 %start.1 = (f32[8,128]{1,0:T(8,128)S(1)}, f32[3,64,128]{2,1,0:T(8,128)S(1)}, f32[3,64,128]{2,1,0:T(8,128)S(1)}, f32[3,48,128]{2,1,0:T(8,128)S(1)}, f32[3,48,128]...) custom-call(s32[1112]{0:T(1024)S(1)} %get-tuple-element.47.control, f32[256,128]{1,0:T(8,128)S(1)} %bitcast.13, ...), custom_call_target="tpu_custom_call" | custom-call | tf_op jit(solution)/shard_map/start/pallas_call | solution.py:606
  41.6 1.6 %collective-permute-start.4 = (f32[3,48,128]{2,1,0:T(8,128)S(1)}, f32[3,48,128]{2,1,0:T(8,128)S(1)}, u32[]{:S(2)}, u32[]{:S(2)}) collective-permute-start(f32[3,48,128]{2,1,0:T(8,128)S(1)} %get-tuple-element.56), channel_id=1, source_target_pairs={{0,32},{1,33},{2,34},{3,35},{4,36},{5,37},{6,38},{7,39},{8,40},{9,... | collective-permute-start | bytes 221192 | tf_op jit(solution)/shard_map/ppermute | solution.py:544
  43.2 1.4 %collective-permute-start.5 = (f32[3,48,128]{2,1,0:T(8,128)S(1)}, f32[3,48,128]{2,1,0:T(8,128)S(1)}, u32[]{:S(2)}, u32[]{:S(2)}) collective-permute-start(f32[3,48,128]{2,1,0:T(8,128)S(1)} %get-tuple-element.57), channel_id=1, source_target_pairs={{0,32},{1,2},{2,1},{3,4},{4,3},{5,6},{6,5},{7,8},{8,7},{9,10},{10,... | collective-permute-start | bytes 221192 | tf_op jit(solution)/shard_map/ppermute | solution.py:544
  44.6 3.5 %collective-permute-start.6 = (f32[3,48,128]{2,1,0:T(8,128)S(1)}, f32[3,48,128]{2,1,0:T(8,128)S(1)}, u32[]{:S(2)}, u32[]{:S(2)}) collective-permute-start(f32[3,48,128]{2,1,0:T(8,128)S(1)} %get-tuple-element.58), channel_id=1, source_target_pairs={{0,1},{1,0},{2,3},{3,2},{4,5},{5,4},{6,7},{7,6},{8,9},{9,8},{10,11... | collective-permute-start | bytes 221192 | tf_op jit(solution)/shard_map/ppermute | solution.py:544
  48.1 6.5 %near_early.4 = (bf16[64,8,16,128]{3,2,1,0:T(8,128)(2,1)S(1)}, f32[512,128]{1,0:T(8,128)S(1)}) custom-call(s32[1112]{0:T(1024)S(1)} %get-tuple-element.47.control, f32[3,64,128]{2,1,0:T(8,128)S(1)} %get-tuple-element.55.own, f32[3,48,128]{2,1,0:T(8,128)S(1)} %collective-permute-done.7.g3, f32[2056,128]{1,0:T(8,128)S(1)} %get-tuple-element.59.burg), custom_call_target="tpu_custom_call" | custom-call | flops 20000000000 | bytes 1048576 | tf_op jit(solution)/shard_map/near_early/pallas_call | solution.py:617
  54.6 6.9 %near_step.3 = (f32[3,64,128]{2,1,0:T(8,128)S(1)}, f32[3,64,128]{2,1,0:T(8,128)S(1)}, f32[3,48,128]{2,1,0:T(8,128)S(1)}, f32[3,48,128]{2,1,0:T(8,128)S(1)}, f32[...) custom-call(s32[1112]{0:T(1024)S(1)} %get-tuple-element.47.control, f32[8,128]{1,0:T(8,128)S(1)} %get-tuple-element.54.expansion, ...), custom_call_target="tpu_custom_call" | custom-call | flops 10000000000 | bytes 1048576 | tf_op jit(solution)/shard_map/near_step/pallas_call | solution.py:627
  61.8 3.6 %collective-permute-start.10 = (f32[3,48,128]{2,1,0:T(8,128)S(1)}, f32[3,48,128]{2,1,0:T(8,128)S(1)}, u32[]{:S(2)}, u32[]{:S(2)}) collective-permute-start(f32[3,48,128]{2,1,0:T(8,128)S(1)} %get-tuple-element.67), channel_id=1, source_target_pairs={{0,1},{1,0},{2,3},{3,2},{4,5},{5,4},{6,7},{7,6},{8,9},{9,8},{10,11... | collective-permute-start | bytes 221192 | tf_op jit(solution)/shard_map/ppermute | solution.py:544
  65.5 6.5 %near_early.5 = (bf16[64,8,16,128]{3,2,1,0:T(8,128)(2,1)S(1)}, f32[512,128]{1,0:T(8,128)S(1)}) custom-call(s32[1112]{0:T(1024)S(1)} %get-tuple-element.47.control, f32[3,64,128]{2,1,0:T(8,128)S(1)} %get-tuple-element.64.own, f32[3,48,128]{2,1,0:T(8,128)S(1)} %collective-permute-done.11.g3, f32[2056,128]{1,0:T(8,128)S(1)} %get-tuple-element.59.burg), custom_call_target="tpu_custom_call" | custom-call | flops 20000000000 | bytes 1048576 | tf_op jit(solution)/shard_map/near_early/pallas_call | solution.py:617
  72.0 6.7 %near_step.4 = (f32[3,64,128]{2,1,0:T(8,128)S(1)}, f32[3,64,128]{2,1,0:T(8,128)S(1)}, f32[3,48,128]{2,1,0:T(8,128)S(1)}, f32[3,48,128]{2,1,0:T(8,128)S(1)}, f32[...) custom-call(s32[1112]{0:T(1024)S(1)} %get-tuple-element.47.control, f32[8,128]{1,0:T(8,128)S(1)} %get-tuple-element.54.expansion, ...), custom_call_target="tpu_custom_call" | custom-call | flops 10000000000 | bytes 1048576 | tf_op jit(solution)/shard_map/near_step/pallas_call | solution.py:627
  79.0 3.3 %collective-permute-start.14 = (f32[3,48,128]{2,1,0:T(8,128)S(1)}, f32[3,48,128]{2,1,0:T(8,128)S(1)}, u32[]{:S(2)}, u32[]{:S(2)}) collective-permute-start(f32[3,48,128]{2,1,0:T(8,128)S(1)} %get-tuple-element.75), channel_id=1, source_target_pairs={{0,1},{1,0},{2,3},{3,2},{4,5},{5,4},{6,7},{7,6},{8,9},{9,8},{10,11... | collective-permute-start | bytes 221192 | tf_op jit(solution)/shard_map/ppermute | solution.py:544
  82.4 6.5 %near_early.6 = (bf16[64,8,16,128]{3,2,1,0:T(8,128)(2,1)S(1)}, f32[512,128]{1,0:T(8,128)S(1)}) custom-call(s32[1112]{0:T(1024)S(1)} %get-tuple-element.47.control, f32[3,64,128]{2,1,0:T(8,128)S(1)} %get-tuple-element.72.own, f32[3,48,128]{2,1,0:T(8,128)S(1)} %collective-permute-done.15.g3, f32[2056,128]{1,0:T(8,128)S(1)} %get-tuple-element.59.burg), custom_call_target="tpu_custom_call" | custom-call | flops 20000000000 | bytes 1048576 | tf_op jit(solution)/shard_map/near_early/pallas_call | solution.py:617
  88.9 7.4 %near_step.5 = (f32[3,8192]{1,0:T(4,128)}, f32[3,64,128]{2,1,0:T(8,128)S(1)}, f32[3,48,128]{2,1,0:T(8,128)S(1)}, f32[3,48,128]{2,1,0:T(8,128)S(1)}, f32[3,48,128...) custom-call(s32[1112]{0:T(1024)S(1)} %get-tuple-element.47.control, f32[8,128]{1,0:T(8,128)S(1)} %get-tuple-element.54.expansion, ...), custom_call_target="tpu_custom_call" | custom-call | flops 10000000000 | bytes 1048576 | tf_op jit(solution)/shard_map/near_step/pallas_call | solution.py:627
  96.4 3.4 %collective-permute-start.18 = (f32[3,48,128]{2,1,0:T(8,128)S(1)}, f32[3,48,128]{2,1,0:T(8,128)S(1)}, u32[]{:S(2)}, u32[]{:S(2)}) collective-permute-start(f32[3,48,128]{2,1,0:T(8,128)S(1)} %get-tuple-element.84), channel_id=1, source_target_pairs={{0,1},{1,0},{2,3},{3,2},{4,5},{5,4},{6,7},{7,6},{8,9},{9,8},{10,11... | collective-permute-start | bytes 221192 | tf_op jit(solution)/shard_map/ppermute | solution.py:544
  99.8 6.4 %near_early.7 = (bf16[64,8,16,128]{3,2,1,0:T(8,128)(2,1)S(1)}, f32[512,128]{1,0:T(8,128)S(1)}) custom-call(s32[1112]{0:T(1024)S(1)} %get-tuple-element.47.control, f32[3,64,128]{2,1,0:T(8,128)S(1)} %get-tuple-element.81.own, f32[3,48,128]{2,1,0:T(8,128)S(1)} %collective-permute-done.19.g3, f32[2056,128]{1,0:T(8,128)S(1)} %get-tuple-element.59.burg), custom_call_target="tpu_custom_call" | custom-call | flops 20000000000 | bytes 1048576 | tf_op jit(solution)/shard_map/near_early/pallas_call | solution.py:617
  106.2 7.0 %near_last.1 = f32[3,8192]{1,0:T(4,128)} custom-call(s32[1112]{0:T(1024)S(1)} %get-tuple-element.47.control, f32[8,128]{1,0:T(8,128)S(1)} %get-tuple-element.54.expansion, f32[3,64,128]{2,1,0:T(8,128)S(1)} %get-tuple-element.81.own, f32[3,48,128]{2,1,0:T(8,128)S(1)} %collective-permute-done.16.g0, f32[3,48,128]{2,1,0:T(8,128)S(1)} %collective-permute-done.17.g2, ...), custom_call_target="tpu_custom_call" | custom-call | flops 10000000000 | bytes 1048576 | tf_op jit(solution)/shard_map/near_last/pallas_call | solution.py:627
  (34 shorter events, 1.5 us)
Async XLA Ops:
  3.9 24.4 %collective-permute-start = (f32[6,48,128]{2,1,0:T(8,128)S(1)}, f32[6,48,128]{2,1,0:T(8,128)S(1)}, u32[]{:S(2)}, u32[]{:S(2)}) collective-permute-start(f32[6,48,128]{2,1,0:T(8,128)S(1)} %get-tuple-element.49), channel_id=1, source_target_pairs={{0,1},{1,0},{2,3},{3,2},{4,5},{5,4},{6,7},{7,6},{8,9},{9,8},{10,11... | collective-permute-start | bytes 442376 | tf_op jit(solution)/shard_map/ppermute | solution.py:544
  4.6 23.7 %collective-permute-start.1 = (f32[6,48,128]{2,1,0:T(8,128)S(1)}, f32[6,48,128]{2,1,0:T(8,128)S(1)}, u32[]{:S(2)}, u32[]{:S(2)}) collective-permute-start(f32[6,48,128]{2,1,0:T(8,128)S(1)} %get-tuple-element.50), channel_id=1, source_target_pairs={{0,32},{1,33},{2,34},{3,35},{4,36},{5,37},{6,38},{7,39},{8,40},{9,... | collective-permute-start | bytes 442376 | tf_op jit(solution)/shard_map/ppermute | solution.py:544
  5.9 22.4 %collective-permute-start.2 = (f32[6,48,128]{2,1,0:T(8,128)S(1)}, f32[6,48,128]{2,1,0:T(8,128)S(1)}, u32[]{:S(2)}, u32[]{:S(2)}) collective-permute-start(f32[6,48,128]{2,1,0:T(8,128)S(1)} %get-tuple-element.51), channel_id=1, source_target_pairs={{0,32},{1,2},{2,1},{3,4},{4,3},{5,6},{6,5},{7,8},{8,7},{9,10},{10,... | collective-permute-start | bytes 442376 | tf_op jit(solution)/shard_map/ppermute | solution.py:544
  9.3 19.0 %collective-permute-start.3 = (f32[6,48,128]{2,1,0:T(8,128)S(1)}, f32[6,48,128]{2,1,0:T(8,128)S(1)}, u32[]{:S(2)}, u32[]{:S(2)}) collective-permute-start(f32[6,48,128]{2,1,0:T(8,128)S(1)} %get-tuple-element.52), channel_id=1, source_target_pairs={{0,1},{1,0},{2,3},{3,2},{4,5},{5,4},{6,7},{7,6},{8,9},{9,8},{10,11... | collective-permute-start | bytes 442376 | tf_op jit(solution)/shard_map/ppermute | solution.py:544
  19.1 21.3 %all-to-all-start = ((f32[256,1,128]{2,1,0:T(1,128)}), f32[256,1,128]{2,1,0:T(1,128)S(1)}, u32[]{:S(2)}, u32[]{:S(2)}) async-start(f32[256,1,128]{2,1,0:T(1,128)} %bitcast.3), calls=%async_computation | async-start | bytes 262144 | tf_op jit(solution)/shard_map/all_to_all | solution.py:592
  28.3 12.0 %copy-start = (f32[8192]{0:T(1024)S(1)}, f32[8192]{0:T(1024)}, u32[]{:S(2)}) copy-start(f32[8192]{0:T(1024)} %param.8) | copy-start | bytes 98308
  41.5 6.6 %collective-permute-start.7 = (f32[3,48,128]{2,1,0:T(8,128)S(1)}, f32[3,48,128]{2,1,0:T(8,128)S(1)}, u32[]{:S(2)}, u32[]{:S(2)}) collective-permute-start(f32[3,48,128]{2,1,0:T(8,128)S(1)} %get-tuple-element.60), channel_id=1, source_target_pairs={{0,1},{1,0},{2,3},{3,2},{4,5},{5,4},{6,7},{7,6},{8,9},{9,8},{10,11... | collective-permute-start | bytes 221192 | tf_op jit(solution)/shard_map/ppermute | solution.py:544
  41.6 13.0 %collective-permute-start.4 = (f32[3,48,128]{2,1,0:T(8,128)S(1)}, f32[3,48,128]{2,1,0:T(8,128)S(1)}, u32[]{:S(2)}, u32[]{:S(2)}) collective-permute-start(f32[3,48,128]{2,1,0:T(8,128)S(1)} %get-tuple-element.56), channel_id=1, source_target_pairs={{0,32},{1,33},{2,34},{3,35},{4,36},{5,37},{6,38},{7,39},{8,40},{9,... | collective-permute-start | bytes 221192 | tf_op jit(solution)/shard_map/ppermute | solution.py:544
  43.2 11.4 %collective-permute-start.5 = (f32[3,48,128]{2,1,0:T(8,128)S(1)}, f32[3,48,128]{2,1,0:T(8,128)S(1)}, u32[]{:S(2)}, u32[]{:S(2)}) collective-permute-start(f32[3,48,128]{2,1,0:T(8,128)S(1)} %get-tuple-element.57), channel_id=1, source_target_pairs={{0,32},{1,2},{2,1},{3,4},{4,3},{5,6},{6,5},{7,8},{8,7},{9,10},{10,... | collective-permute-start | bytes 221192 | tf_op jit(solution)/shard_map/ppermute | solution.py:544
  44.6 10.0 %collective-permute-start.6 = (f32[3,48,128]{2,1,0:T(8,128)S(1)}, f32[3,48,128]{2,1,0:T(8,128)S(1)}, u32[]{:S(2)}, u32[]{:S(2)}) collective-permute-start(f32[3,48,128]{2,1,0:T(8,128)S(1)} %get-tuple-element.58), channel_id=1, source_target_pairs={{0,1},{1,0},{2,3},{3,2},{4,5},{5,4},{6,7},{7,6},{8,9},{9,8},{10,11... | collective-permute-start | bytes 221192 | tf_op jit(solution)/shard_map/ppermute | solution.py:544
  61.5 3.9 %collective-permute-start.11 = (f32[3,48,128]{2,1,0:T(8,128)S(1)}, f32[3,48,128]{2,1,0:T(8,128)S(1)}, u32[]{:S(2)}, u32[]{:S(2)}) collective-permute-start(f32[3,48,128]{2,1,0:T(8,128)S(1)} %get-tuple-element.68), channel_id=1, source_target_pairs={{0,1},{1,0},{2,3},{3,2},{4,5},{5,4},{6,7},{7,6},{8,9},{9,8},{10,11... | collective-permute-start | bytes 221192 | tf_op jit(solution)/shard_map/ppermute | solution.py:544
  61.6 10.3 %collective-permute-start.8 = (f32[3,48,128]{2,1,0:T(8,128)S(1)}, f32[3,48,128]{2,1,0:T(8,128)S(1)}, u32[]{:S(2)}, u32[]{:S(2)}) collective-permute-start(f32[3,48,128]{2,1,0:T(8,128)S(1)} %get-tuple-element.65), channel_id=1, source_target_pairs={{0,32},{1,33},{2,34},{3,35},{4,36},{5,37},{6,38},{7,39},{8,40},{9,... | collective-permute-start | bytes 221192 | tf_op jit(solution)/shard_map/ppermute | solution.py:544
  61.7 10.2 %collective-permute-start.9 = (f32[3,48,128]{2,1,0:T(8,128)S(1)}, f32[3,48,128]{2,1,0:T(8,128)S(1)}, u32[]{:S(2)}, u32[]{:S(2)}) collective-permute-start(f32[3,48,128]{2,1,0:T(8,128)S(1)} %get-tuple-element.66), channel_id=1, source_target_pairs={{0,32},{1,2},{2,1},{3,4},{4,3},{5,6},{6,5},{7,8},{8,7},{9,10},{10,... | collective-permute-start | bytes 221192 | tf_op jit(solution)/shard_map/ppermute | solution.py:544
  61.8 10.1 %collective-permute-start.10 = (f32[3,48,128]{2,1,0:T(8,128)S(1)}, f32[3,48,128]{2,1,0:T(8,128)S(1)}, u32[]{:S(2)}, u32[]{:S(2)}) collective-permute-start(f32[3,48,128]{2,1,0:T(8,128)S(1)} %get-tuple-element.67), channel_id=1, source_target_pairs={{0,1},{1,0},{2,3},{3,2},{4,5},{5,4},{6,7},{7,6},{8,9},{9,8},{10,11... | collective-permute-start | bytes 221192 | tf_op jit(solution)/shard_map/ppermute | solution.py:544
  78.7 3.6 %collective-permute-start.15 = (f32[3,48,128]{2,1,0:T(8,128)S(1)}, f32[3,48,128]{2,1,0:T(8,128)S(1)}, u32[]{:S(2)}, u32[]{:S(2)}) collective-permute-start(f32[3,48,128]{2,1,0:T(8,128)S(1)} %get-tuple-element.76), channel_id=1, source_target_pairs={{0,1},{1,0},{2,3},{3,2},{4,5},{5,4},{6,7},{7,6},{8,9},{9,8},{10,11... | collective-permute-start | bytes 221192 | tf_op jit(solution)/shard_map/ppermute | solution.py:544
  78.8 10.0 %collective-permute-start.12 = (f32[3,48,128]{2,1,0:T(8,128)S(1)}, f32[3,48,128]{2,1,0:T(8,128)S(1)}, u32[]{:S(2)}, u32[]{:S(2)}) collective-permute-start(f32[3,48,128]{2,1,0:T(8,128)S(1)} %get-tuple-element.73), channel_id=1, source_target_pairs={{0,32},{1,33},{2,34},{3,35},{4,36},{5,37},{6,38},{7,39},{8,40},{9,... | collective-permute-start | bytes 221192 | tf_op jit(solution)/shard_map/ppermute | solution.py:544
  78.9 9.9 %collective-permute-start.13 = (f32[3,48,128]{2,1,0:T(8,128)S(1)}, f32[3,48,128]{2,1,0:T(8,128)S(1)}, u32[]{:S(2)}, u32[]{:S(2)}) collective-permute-start(f32[3,48,128]{2,1,0:T(8,128)S(1)} %get-tuple-element.74), channel_id=1, source_target_pairs={{0,32},{1,2},{2,1},{3,4},{4,3},{5,6},{6,5},{7,8},{8,7},{9,10},{10,... | collective-permute-start | bytes 221192 | tf_op jit(solution)/shard_map/ppermute | solution.py:544
  79.0 9.8 %collective-permute-start.14 = (f32[3,48,128]{2,1,0:T(8,128)S(1)}, f32[3,48,128]{2,1,0:T(8,128)S(1)}, u32[]{:S(2)}, u32[]{:S(2)}) collective-permute-start(f32[3,48,128]{2,1,0:T(8,128)S(1)} %get-tuple-element.75), channel_id=1, source_target_pairs={{0,1},{1,0},{2,3},{3,2},{4,5},{5,4},{6,7},{7,6},{8,9},{9,8},{10,11... | collective-permute-start | bytes 221192 | tf_op jit(solution)/shard_map/ppermute | solution.py:544
  96.3 3.5 %collective-permute-start.19 = (f32[3,48,128]{2,1,0:T(8,128)S(1)}, f32[3,48,128]{2,1,0:T(8,128)S(1)}, u32[]{:S(2)}, u32[]{:S(2)}) collective-permute-start(f32[3,48,128]{2,1,0:T(8,128)S(1)} %get-tuple-element.85), channel_id=1, source_target_pairs={{0,1},{1,0},{2,3},{3,2},{4,5},{5,4},{6,7},{7,6},{8,9},{9,8},{10,11... | collective-permute-start | bytes 221192 | tf_op jit(solution)/shard_map/ppermute | solution.py:544
  96.3 9.9 %collective-permute-start.16 = (f32[3,48,128]{2,1,0:T(8,128)S(1)}, f32[3,48,128]{2,1,0:T(8,128)S(1)}, u32[]{:S(2)}, u32[]{:S(2)}) collective-permute-start(f32[3,48,128]{2,1,0:T(8,128)S(1)} %get-tuple-element.82), channel_id=1, source_target_pairs={{0,32},{1,33},{2,34},{3,35},{4,36},{5,37},{6,38},{7,39},{8,40},{9,... | collective-permute-start | bytes 221192 | tf_op jit(solution)/shard_map/ppermute | solution.py:544
  96.3 9.9 %collective-permute-start.17 = (f32[3,48,128]{2,1,0:T(8,128)S(1)}, f32[3,48,128]{2,1,0:T(8,128)S(1)}, u32[]{:S(2)}, u32[]{:S(2)}) collective-permute-start(f32[3,48,128]{2,1,0:T(8,128)S(1)} %get-tuple-element.83), channel_id=1, source_target_pairs={{0,32},{1,2},{2,1},{3,4},{4,3},{5,6},{6,5},{7,8},{8,7},{9,10},{10,... | collective-permute-start | bytes 221192 | tf_op jit(solution)/shard_map/ppermute | solution.py:544
  96.4 9.8 %collective-permute-start.18 = (f32[3,48,128]{2,1,0:T(8,128)S(1)}, f32[3,48,128]{2,1,0:T(8,128)S(1)}, u32[]{:S(2)}, u32[]{:S(2)}) collective-permute-start(f32[3,48,128]{2,1,0:T(8,128)S(1)} %get-tuple-element.84), channel_id=1, source_target_pairs={{0,1},{1,0},{2,3},{3,2},{4,5},{5,4},{6,7},{7,6},{8,9},{9,8},{10,11... | collective-permute-start | bytes 221192 | tf_op jit(solution)/shard_map/ppermute | solution.py:544
where the time goes:
time: 114 us; the launch traced here: 113 us
  Pallas kernels  75.9 us (67%)
  starting transfers between devices  34.6 us (30%)
    pallas_call x4, Pallas kernels, evaluate(): pl.pallas_call(kernel, out_shape=out_shape, in_specs=[smem] + [vmem] * (6...  28.1 us
    pallas_call x4, Pallas kernels, evaluate(): pl.pallas_call(early_kernel, out_shape=[shape(*right_shape, dtype=bf16),...  25.8 us
    ppermute x20, starting transfers between devices, swap(): return lax.ppermute(x, ('slab', 'cell'), pairs)  25.5 us
    pallas_call x1, Pallas kernels, local(): pl.pallas_call(first_kernel, out_shape=[block, shape((EXT + 1) * 8, LANES...  12 us
    all_to_all x1, starting transfers between devices, local(): shares = lax.all_to_all(shares, ('slab', 'cell'), 0, 0, tiled=True)  9.17 us
    pallas_call x1, Pallas kernels, local(): pl.pallas_call(far_kernel, out_shape=[shape(EXT, LANES), shape(CONTROL, d...  7.33 us
  transfers between devices with their start and end apart: 21, of which 0 were waited for; matrix products, arithmetic and copies ran while one was open for 0% of the time, Pallas kernels for 40%

commit v1 on v0

--- a/solution.py
+++ b/solution.py
@@ -31,7 +31,6 @@
 bf16 = jnp.bfloat16
 
 vmem = pl.BlockSpec(memory_space=pltpu.VMEM)
-smem = pl.BlockSpec(memory_space=pltpu.SMEM)
 params = pltpu.CompilerParams(vmem_limit_bytes=40 * 2**20)
 
 
@@ -157,7 +156,11 @@
     return words, amounts
 
 
-def pack_kernel(numbers_smem, numbers, positions, burgers, places, scalars, s3, s0, s2, s1):
+def pack_kernel(
+    numbers, positions, burgers, places, scalars, s3, s0, s2, s1, numbers_smem, sem
+):
+    copy = pltpu.make_async_copy(numbers, numbers_smem, sem)
+    copy.start()
     slab, cell = centre_of()
     for k, by in enumerate((slab + 0.5, cell + 0.5, 0.5)):
         places[k] = positions[k] - by
@@ -173,6 +176,7 @@
             rows[d] == first, numbers[8 + first : 9 + first, :], numbers[9 + first : 10 + first, :]
         )
     sources = [(places, k) for k in range(3)] + [(burgers, a) for a in range(3)]
+    copy.wait()
     fill_sends(lambda d, n: numbers_smem[8 + rows[d], n], sources, {0: s0, 1: s1, 2: s2, 3: s3})
 
 
@@ -197,9 +201,11 @@
 
 
 def far_kernel(
-    scalars, places, burgers, out, control, acc, rows, cols, apart_by, w_even, w_odd
+    scalars_in, places, burgers, out, control_out, acc, rows, cols, apart_by, w_even, w_odd,
+    scalars, control, sems
 ):
-    amounts = [scalars[NEAR, 0], scalars[NEAR + 1, 0]]
+    copy = pltpu.make_async_copy(scalars_in, scalars, sems.at[0])
+    copy.start()
     for i in range(LEAD):
         control[AT_PAIRS - LEAD + i] = EXT
         control[AT_PAIRS + LIST - LEAD + i] = EXT
@@ -264,18 +270,23 @@
                 w_now[g, :LANES, EXT * k : EXT * k + EXT] = high
                 w_now[g, LANES:, EXT * k : EXT * k + EXT] = low
 
+    copy.wait()
+
     def body(step, carry):
         half(2 * step, w_even, w_odd)
         half(2 * step + 1, w_odd, w_even)
         return carry
 
     lax.fori_loop(0, BLOCKS // 8, body, 0)
-    for g in range(4):
-        sums(BLOCKS // 4 - 1, g, w_odd)
+    amounts = [scalars[NEAR, 0], scalars[NEAR + 1, 0]]
     for k in range(2):
         for i in range(TAIL):
             control[AT_PAIRS + LIST * k + amounts[k] + i] = EXT
         control[k] = amounts[k]
+    copy = pltpu.make_async_copy(control, control_out, sems.at[1])
+    copy.start()
+    for g in range(4):
+        sums(BLOCKS // 4 - 1, g, w_odd)
 
     apart = apart + [jnp.zeros((1, EXT), f32)]
 
@@ -292,6 +303,7 @@
     zero = jnp.zeros((LANES - 12, 2 * LANES), f32)
     values = jnp.concatenate(direct + gradient + [zero], axis=0)
     out[...] = jnp.concatenate([values[:, :LANES].T, values[:, LANES:].T], axis=0)
+    copy.wait()
 
 
 def tile_of(own, ghosts, index, tile):
@@ -421,7 +433,8 @@
 parts_scratch = pltpu.VMEM((12, BLOCKS, LANES), f32)
 right_shape = (BLOCKS, 8, 16, LANES)
 acc_shape = (BLOCKS * 8, LANES)
-near_scratch = [
+control_scratch = [pltpu.SMEM((CONTROL,), jnp.int32), pltpu.SemaphoreType.DMA]
+near_scratch = control_scratch + [
     pltpu.VMEM((EXT // 4 + 1, LANES, LANES), bf16),
     pltpu.VMEM((4, 16, LANES), bf16),
     pltpu.VMEM((GROUP, 2 * LANES, LANES), bf16),
@@ -440,8 +453,10 @@
 
 
 def first_kernel(
-    control, own, burgers, g3, g0, g2, g1, near, burg, left, mask, k_even, k_odd, parts, right, acc
+    control_in, own, burgers, g3, g0, g2, g1, near, burg, control, sem, left, mask, k_even, k_odd, parts, right, acc
 ):
+    copy = pltpu.make_async_copy(control_in, control, sem)
+    copy.start()
     ghosts = (g0, g1, g2, g3)
     exists = slot_exists()
     burg[...] = jnp.zeros_like(burg)
@@ -460,13 +475,18 @@
     prepare_sources(own, ghosts, range(EXT // 8), left)
     prepare_targets(own, parts, right)
     acc[...] = jnp.zeros_like(acc)
+    copy.wait()
     for which in range(2):
         add_pairs(control, which, burg, left, right, mask, acc, k_even, k_odd)
     for a in range(3):
         near[a] = component(acc, a)
 
 
-def start_kernel(control, shares, near, places, mobility, expansion, moved, now, *sends):
+def start_kernel(
+    control_in, shares, near, places, mobility, expansion, moved, now, s0, s1, s2, s3, control, sem
+):
+    copy = pltpu.make_async_copy(control_in, control, sem)
+    copy.start()
     expansion[...] = jnp.broadcast_to(jnp.sum(shares[...], axis=0, keepdims=True), (8, LANES))
     p = [places[k] for k in range(3)]
     force = total_force(expansion[...], [near[a] for a in range(3)], p)
@@ -474,20 +494,31 @@
         step = (time_step * mobility[...]) * force[a]
         moved[a] = step
         now[a] = p[a] + step
-    send_now(control, now, sends)
-
-
-def early_kernel(control, own, g3, burg, right, acc, left, mask, k_even, k_odd, parts):
+    copy.wait()
+    send_now(control, now, (s0, s1, s2, s3))
+
+
+def early_kernel(
+    control_in, own, g3, burg, right, acc, control, sem, left, mask, k_even, k_odd, parts
+):
+    copy = pltpu.make_async_copy(control_in, control, sem)
+    copy.start()
     ghosts = (None, None, None, g3)
     prepare_sources(own, ghosts, list(range(BLOCKS // 8)) + tiles_of(EARLY), left)
     prepare_targets(own, parts, right)
     acc[...] = jnp.zeros_like(acc)
+    copy.wait()
     add_pairs(control, 0, burg, left, right, mask, acc, k_even, k_odd)
 
 
-def late_force(control, expansion, own, g0, g2, g1, burg, right, acc_in, left, mask, k_even, k_odd, acc):
+def late_force(
+    control_in, expansion, own, g0, g2, g1, burg, right, acc_in, control, sem, left, mask, k_even, k_odd, acc
+):
+    copy = pltpu.make_async_copy(control_in, control, sem)
+    copy.start()
     prepare_sources(own, (g0, g1, g2, None), tiles_of(LATE), left)
     acc[...] = acc_in[...]
+    copy.wait()
     add_pairs(control, 1, burg, left, right, mask, acc, k_even, k_odd)
     return total_force(
         expansion[...], [component(acc, a) for a in range(3)], [own[k] for k in range(3)]
@@ -506,7 +537,7 @@
         else:
             new_moved[a] = total
         now[a] = places[a] + total
-    send_now(control, now, (s0, s1, s2, s3))
+    send_now(scratch[0], now, (s0, s1, s2, s3))
 
 
 def last_kernel(
@@ -565,18 +596,19 @@
     places, scalars, *sends = pl.pallas_call(
         pack_kernel,
         out_shape=[block, shape(16, LANES, dtype=jnp.int32)] + [shape(6, GHOST, LANES)] * 4,
-        in_specs=[smem, vmem, vmem, vmem],
+        in_specs=[vmem] * 3,
         out_specs=[vmem] * 6,
+        scratch_shapes=[pltpu.SMEM((16, LANES), jnp.int32), pltpu.SemaphoreType.DMA],
         compiler_params=params,
         name="pack",
-    )(numbers, numbers, positions, burgers)
+    )(numbers, positions, burgers)
     ghosts = [swap(x, slot) for x, slot in zip(sends, (3, 0, 2, 1))]
 
     shares, control = pl.pallas_call(
         far_kernel,
         out_shape=[shape(EXT, LANES), shape(CONTROL, dtype=jnp.int32)],
-        in_specs=[smem, vmem, vmem],
-        out_specs=[vmem, smem],
+        in_specs=[vmem] * 3,
+        out_specs=[vmem] * 2,
         scratch_shapes=[
             pltpu.VMEM((32, 2 * EXT), f32),
             pltpu.VMEM((BLOCKS // 4, LANES, LANES), f32),
@@ -584,6 +616,9 @@
             pltpu.VMEM((4, LANES, EXT), bf16),
             pltpu.VMEM((4, 2 * LANES, 2 * EXT), bf16),
             pltpu.VMEM((4, 2 * LANES, 2 * EXT), bf16),
+            pltpu.SMEM((16, LANES), jnp.int32),
+            pltpu.SMEM((CONTROL,), jnp.int32),
+            pltpu.SemaphoreType.DMA((2,)),
         ],
         compiler_params=params,
         cost_estimate=cost(20e9),
@@ -594,7 +629,7 @@
     near, burg = pl.pallas_call(
         first_kernel,
         out_shape=[block, shape((EXT + 1) * 8, LANES)],
-        in_specs=[smem] + [vmem] * 6,
+        in_specs=[vmem] * 7,
         out_specs=[vmem] * 2,
         scratch_shapes=near_scratch
         + [parts_scratch, pltpu.VMEM(right_shape, bf16), pltpu.VMEM(acc_shape, f32)],
@@ -606,8 +641,9 @@
     expansion, moved, now, *sends = pl.pallas_call(
         start_kernel,
         out_shape=[shape(8, LANES), block, block] + [send] * 4,
-        in_specs=[smem] + [vmem] * 4,
+        in_specs=[vmem] * 5,
         out_specs=[vmem] * 7,
+        scratch_shapes=control_scratch,
         compiler_params=params,
         name="start",
     )(control, shares, near, places, mobility)
@@ -617,7 +653,7 @@
         right, acc = pl.pallas_call(
             early_kernel,
             out_shape=[shape(*right_shape, dtype=bf16), shape(*acc_shape)],
-            in_specs=[smem] + [vmem] * 3,
+            in_specs=[vmem] * 4,
             out_specs=[vmem] * 2,
             scratch_shapes=near_scratch + [parts_scratch],
             compiler_params=params,
@@ -627,7 +663,7 @@
         return pl.pallas_call(
             kernel,
             out_shape=out_shape,
-            in_specs=[smem] + [vmem] * (6 + len(LATE) + len(more)),
+            in_specs=[vmem] * (7 + len(LATE) + len(more)),
             out_specs=jax.tree.map(lambda _: vmem, out_shape),
             scratch_shapes=near_scratch + [pltpu.VMEM(acc_shape, f32)],
             compiler_params=params,

time: 114 us -> 107 us (0.939)
  the two profiles are of different devices: /device:TPU:103 before, /device:TPU:9 now
where the time goes in v1:
time: 107 us; the launch traced here: 108 us
  Pallas kernels  71.3 us (67%)
  starting transfers between devices  33.5 us (31%)
  between operations  1.1 us (1%)
    pallas_call x4, Pallas kernels, evaluate(): pl.pallas_call(kernel, out_shape=out_shape, in_specs=[vmem] * (7 + len(LA...  31.8 us
    ppermute x20, starting transfers between devices, swap(): return lax.ppermute(x, ('slab', 'cell'), pairs)  20.4 us
    pallas_call x4, Pallas kernels, evaluate(): pl.pallas_call(early_kernel, out_shape=[shape(*right_shape, dtype=bf16),...  18.5 us
    all_to_all x1, starting transfers between devices, local(): shares = lax.all_to_all(shares, ('slab', 'cell'), 0, 0, tiled=True)  13.1 us
    pallas_call x1, Pallas kernels, local(): pl.pallas_call(first_kernel, out_shape=[block, shape((EXT + 1) * 8, LANES...  11.4 us
    pallas_call x1, Pallas kernels, local(): pl.pallas_call(far_kernel, out_shape=[shape(EXT, LANES), shape(CONTROL, d...  7.12 us
  transfers between devices with their start and end apart: 21, of which 1 were waited for; matrix products, arithmetic and copies ran while one was open for 0% of the time, Pallas kernels for 34%

profile of v1, /device:TPU:9, one launch (start us, length us, event | category | flops | bytes accessed | tf_op | source)
XLA Modules:
  0.0 107.7 jit_solution(5681010959179047753)
XLA Ops:
  0.6 1.0 copy_bitcast_fusion
  2.3 1.4 %pack.1 = (f32[3,64,128]{2,1,0:T(8,128)S(1)}, s32[16,128]{1,0:T(8,128)S(1)}, f32[6,48,128]{2,1,0:T(8,128)S(1)}, f32[6,48,128]{2,1,0:T(8,128)S(1)}, f32[6,48,128]{2,1,0:T(8,128)S(1)}, /*index=5*/f32[6,48,128]{2,1,0:T(8,128)S(1)}) custom-call(s32[16,128]{1,0:T(8,128)S(1)} %pad_add_fusion.numbers, f32[3,64,128]{2,1,0:T(8,128)S(1)} %get-tuple-element.89.positions, ...), custom_call_target="tpu_custom_call" | custom-call | tf_op jit(solution)/shard_map/pack/pallas_call | solution.py:596
  4.5 1.9 %collective-permute-start.1 = (f32[6,48,128]{2,1,0:T(8,128)S(1)}, f32[6,48,128]{2,1,0:T(8,128)S(1)}, u32[]{:S(2)}, u32[]{:S(2)}) collective-permute-start(f32[6,48,128]{2,1,0:T(8,128)S(1)} %get-tuple-element.50), channel_id=1, source_target_pairs={{0,32},{1,33},{2,34},{3,35},{4,36},{5,37},{6,38},{7,39},{8,40},{9,... | collective-permute-start | bytes 442376 | tf_op jit(solution)/shard_map/ppermute | solution.py:575
  6.4 1.8 %collective-permute-start.3 = (f32[6,48,128]{2,1,0:T(8,128)S(1)}, f32[6,48,128]{2,1,0:T(8,128)S(1)}, u32[]{:S(2)}, u32[]{:S(2)}) collective-permute-start(f32[6,48,128]{2,1,0:T(8,128)S(1)} %get-tuple-element.52), channel_id=1, source_target_pairs={{0,1},{1,0},{2,3},{3,2},{4,5},{5,4},{6,7},{7,6},{8,9},{9,8},{10,11... | collective-permute-start | bytes 442376 | tf_op jit(solution)/shard_map/ppermute | solution.py:575
  8.3 7.1 %far.1 = (f32[256,128]{1,0:T(8,128)}, s32[1112]{0:T(1024)S(1)}) custom-call(s32[16,128]{1,0:T(8,128)S(1)} %get-tuple-element.45.scalars_in, f32[3,64,128]{2,1,0:T(8,128)S(1)} %get-tuple-element.46.places.own, f32[3,64,128]{2,1,0:T(8,128)S(1)} %get-tuple-element.88.burgers), custom_call_target="tpu_custom_call" | custom-call | flops 20000000000 | bytes 1048576 | tf_op jit(solution)/shard_map/far/pallas_call | solution.py:607
  15.4 13.1 %all-to-all-start = ((f32[256,1,128]{2,1,0:T(1,128)}), f32[256,1,128]{2,1,0:T(1,128)S(1)}, u32[]{:S(2)}, u32[]{:S(2)}) async-start(f32[256,1,128]{2,1,0:T(1,128)} %bitcast.3), calls=%async_computation | async-start | bytes 262144 | tf_op jit(solution)/shard_map/all_to_all | solution.py:627
  28.6 11.4 %near_first.1 = (f32[3,64,128]{2,1,0:T(8,128)S(1)}, f32[2056,128]{1,0:T(8,128)S(1)}) custom-call(s32[1112]{0:T(1024)S(1)} %get-tuple-element.47.control_in.control, f32[3,64,128]{2,1,0:T(8,128)S(1)} %get-tuple-element.46.places.own, f32[3,64,128]{2,1,0:T(8,128)S(1)} %get-tuple-element.88.burgers, f32[6,48,128]{2,1,0:T(8,128)S(1)} %collective-permute-done.g3, ...), custom_call_target="tpu_custom_call" | custom-call | flops 20000000000 | bytes 1048576 | tf_op jit(solution)/shard_map/near_first/pallas_call | solution.py:629
  40.1 1.0 start.1
  41.1 1.2 %collective-permute-start.7 = (f32[3,48,128]{2,1,0:T(8,128)S(1)}, f32[3,48,128]{2,1,0:T(8,128)S(1)}, u32[]{:S(2)}, u32[]{:S(2)}) collective-permute-start(f32[3,48,128]{2,1,0:T(8,128)S(1)} %get-tuple-element.60), channel_id=1, source_target_pairs={{0,1},{1,0},{2,3},{3,2},{4,5},{5,4},{6,7},{7,6},{8,9},{9,8},{10,11... | collective-permute-start | bytes 221192 | tf_op jit(solution)/shard_map/ppermute | solution.py:575
  42.3 1.1 %collective-permute-start.4 = (f32[3,48,128]{2,1,0:T(8,128)S(1)}, f32[3,48,128]{2,1,0:T(8,128)S(1)}, u32[]{:S(2)}, u32[]{:S(2)}) collective-permute-start(f32[3,48,128]{2,1,0:T(8,128)S(1)} %get-tuple-element.56), channel_id=1, source_target_pairs={{0,32},{1,33},{2,34},{3,35},{4,36},{5,37},{6,38},{7,39},{8,40},{9,... | collective-permute-start | bytes 221192 | tf_op jit(solution)/shard_map/ppermute | solution.py:575
  44.5 4.7 %near_early.4 = (bf16[64,8,16,128]{3,2,1,0:T(8,128)(2,1)S(1)}, f32[512,128]{1,0:T(8,128)S(1)}) custom-call(s32[1112]{0:T(1024)S(1)} %get-tuple-element.47.control_in.control, f32[3,64,128]{2,1,0:T(8,128)S(1)} %get-tuple-element.55.own, f32[3,48,128]{2,1,0:T(8,128)S(1)} %collective-permute-done.7.g3, f32[2056,128]{1,0:T(8,128)S(1)} %get-tuple-element.59.burg), custom_call_target="tpu_custom_call" | custom-call | flops 20000000000 | bytes 1048576 | tf_op jit(solution)/shard_map/near_early/pallas_call | solution.py:653
  49.2 7.8 %near_step.3 = (f32[3,64,128]{2,1,0:T(8,128)S(1)}, f32[3,64,128]{2,1,0:T(8,128)S(1)}, f32[3,48,128]{2,1,0:T(8,128)S(1)}, f32[3,48,128]{2,1,0:T(8,128)S(1)}, f32[...) custom-call(s32[1112]{0:T(1024)S(1)} %get-tuple-element.47.control_in.control, ...), custom_call_target="tpu_custom_call" | custom-call | flops 10000000000 | bytes 1048576 | tf_op jit(solution)/shard_map/near_step/pallas_call | solution.py:663
  57.2 3.0 %collective-permute-start.9 = (f32[3,48,128]{2,1,0:T(8,128)S(1)}, f32[3,48,128]{2,1,0:T(8,128)S(1)}, u32[]{:S(2)}, u32[]{:S(2)}) collective-permute-start(f32[3,48,128]{2,1,0:T(8,128)S(1)} %get-tuple-element.66), channel_id=1, source_target_pairs={{0,32},{1,2},{2,1},{3,4},{4,3},{5,6},{6,5},{7,8},{8,7},{9,10},{10,... | collective-permute-start | bytes 221192 | tf_op jit(solution)/shard_map/ppermute | solution.py:575
  60.2 1.5 %collective-permute-start.10 = (f32[3,48,128]{2,1,0:T(8,128)S(1)}, f32[3,48,128]{2,1,0:T(8,128)S(1)}, u32[]{:S(2)}, u32[]{:S(2)}) collective-permute-start(f32[3,48,128]{2,1,0:T(8,128)S(1)} %get-tuple-element.67), channel_id=1, source_target_pairs={{0,1},{1,0},{2,3},{3,2},{4,5},{5,4},{6,7},{7,6},{8,9},{9,8},{10,11... | collective-permute-start | bytes 221192 | tf_op jit(solution)/shard_map/ppermute | solution.py:575
  61.8 4.7 %near_early.5 = (bf16[64,8,16,128]{3,2,1,0:T(8,128)(2,1)S(1)}, f32[512,128]{1,0:T(8,128)S(1)}) custom-call(s32[1112]{0:T(1024)S(1)} %get-tuple-element.47.control_in.control, f32[3,64,128]{2,1,0:T(8,128)S(1)} %get-tuple-element.64.own, f32[3,48,128]{2,1,0:T(8,128)S(1)} %collective-permute-done.11.g3, f32[2056,128]{1,0:T(8,128)S(1)} %get-tuple-element.59.burg), custom_call_target="tpu_custom_call" | custom-call | flops 20000000000 | bytes 1048576 | tf_op jit(solution)/shard_map/near_early/pallas_call | solution.py:653
  66.4 7.7 %near_step.4 = (f32[3,64,128]{2,1,0:T(8,128)S(1)}, f32[3,64,128]{2,1,0:T(8,128)S(1)}, f32[3,48,128]{2,1,0:T(8,128)S(1)}, f32[3,48,128]{2,1,0:T(8,128)S(1)}, f32[...) custom-call(s32[1112]{0:T(1024)S(1)} %get-tuple-element.47.control_in.control, ...), custom_call_target="tpu_custom_call" | custom-call | flops 10000000000 | bytes 1048576 | tf_op jit(solution)/shard_map/near_step/pallas_call | solution.py:663
  74.3 3.0 %collective-permute-start.13 = (f32[3,48,128]{2,1,0:T(8,128)S(1)}, f32[3,48,128]{2,1,0:T(8,128)S(1)}, u32[]{:S(2)}, u32[]{:S(2)}) collective-permute-start(f32[3,48,128]{2,1,0:T(8,128)S(1)} %get-tuple-element.74), channel_id=1, source_target_pairs={{0,32},{1,2},{2,1},{3,4},{4,3},{5,6},{6,5},{7,8},{8,7},{9,10},{10,... | collective-permute-start | bytes 221192 | tf_op jit(solution)/shard_map/ppermute | solution.py:575
  77.3 1.3 %collective-permute-start.14 = (f32[3,48,128]{2,1,0:T(8,128)S(1)}, f32[3,48,128]{2,1,0:T(8,128)S(1)}, u32[]{:S(2)}, u32[]{:S(2)}) collective-permute-start(f32[3,48,128]{2,1,0:T(8,128)S(1)} %get-tuple-element.75), channel_id=1, source_target_pairs={{0,1},{1,0},{2,3},{3,2},{4,5},{5,4},{6,7},{7,6},{8,9},{9,8},{10,11... | collective-permute-start | bytes 221192 | tf_op jit(solution)/shard_map/ppermute | solution.py:575
  78.6 4.7 %near_early.6 = (bf16[64,8,16,128]{3,2,1,0:T(8,128)(2,1)S(1)}, f32[512,128]{1,0:T(8,128)S(1)}) custom-call(s32[1112]{0:T(1024)S(1)} %get-tuple-element.47.control_in.control, f32[3,64,128]{2,1,0:T(8,128)S(1)} %get-tuple-element.72.own, f32[3,48,128]{2,1,0:T(8,128)S(1)} %collective-permute-done.15.g3, f32[2056,128]{1,0:T(8,128)S(1)} %get-tuple-element.59.burg), custom_call_target="tpu_custom_call" | custom-call | flops 20000000000 | bytes 1048576 | tf_op jit(solution)/shard_map/near_early/pallas_call | solution.py:653
  83.3 8.5 %near_step.5 = (f32[3,8192]{1,0:T(4,128)}, f32[3,64,128]{2,1,0:T(8,128)S(1)}, f32[3,48,128]{2,1,0:T(8,128)S(1)}, f32[3,48,128]{2,1,0:T(8,128)S(1)}, f32[3,48,128...) custom-call(s32[1112]{0:T(1024)S(1)} %get-tuple-element.47.control_in.control, f32[8,128]{1,0:T(8,128)S(1)} %get-tuple-element.54.expansion, ...), custom_call_target="tpu_custom_call" | custom-call | flops 10000000000 | bytes 1048576 | tf_op jit(solution)/shard_map/near_step/pallas_call | solution.py:663
  92.0 1.3 %collective-permute-start.17 = (f32[3,48,128]{2,1,0:T(8,128)S(1)}, f32[3,48,128]{2,1,0:T(8,128)S(1)}, u32[]{:S(2)}, u32[]{:S(2)}) collective-permute-start(f32[3,48,128]{2,1,0:T(8,128)S(1)} %get-tuple-element.83), channel_id=1, source_target_pairs={{0,32},{1,2},{2,1},{3,4},{4,3},{5,6},{6,5},{7,8},{8,7},{9,10},{10,... | collective-permute-start | bytes 221192 | tf_op jit(solution)/shard_map/ppermute | solution.py:575
  93.3 1.8 %collective-permute-start.18 = (f32[3,48,128]{2,1,0:T(8,128)S(1)}, f32[3,48,128]{2,1,0:T(8,128)S(1)}, u32[]{:S(2)}, u32[]{:S(2)}) collective-permute-start(f32[3,48,128]{2,1,0:T(8,128)S(1)} %get-tuple-element.84), channel_id=1, source_target_pairs={{0,1},{1,0},{2,3},{3,2},{4,5},{5,4},{6,7},{7,6},{8,9},{9,8},{10,11... | collective-permute-start | bytes 221192 | tf_op jit(solution)/shard_map/ppermute | solution.py:575
  95.1 4.6 %near_early.7 = (bf16[64,8,16,128]{3,2,1,0:T(8,128)(2,1)S(1)}, f32[512,128]{1,0:T(8,128)S(1)}) custom-call(s32[1112]{0:T(1024)S(1)} %get-tuple-element.47.control_in.control, f32[3,64,128]{2,1,0:T(8,128)S(1)} %get-tuple-element.81.own, f32[3,48,128]{2,1,0:T(8,128)S(1)} %collective-permute-done.19.g3, f32[2056,128]{1,0:T(8,128)S(1)} %get-tuple-element.59.burg), custom_call_target="tpu_custom_call" | custom-call | flops 20000000000 | bytes 1048576 | tf_op jit(solution)/shard_map/near_early/pallas_call | solution.py:653
  99.7 7.8 %near_last.1 = f32[3,8192]{1,0:T(4,128)} custom-call(s32[1112]{0:T(1024)S(1)} %get-tuple-element.47.control_in.control, f32[8,128]{1,0:T(8,128)S(1)} %get-tuple-element.54.expansion, f32[3,64,128]{2,1,0:T(8,128)S(1)} %get-tuple-element.81.own, f32[3,48,128]{2,1,0:T(8,128)S(1)} %collective-permute-done.16.g0, f32[3,48,128]{2,1,0:T(8,128)S(1)} %collective-permute-done.17.g2, ...), custom_call_target="tpu_custom_call" | custom-call | flops 10000000000 | bytes 1048576 | tf_op jit(solution)/shard_map/near_last/pallas_call | solution.py:663
  (34 shorter events, 3.2 us)
Async XLA Ops:
  3.7 24.8 %collective-permute-start = (f32[6,48,128]{2,1,0:T(8,128)S(1)}, f32[6,48,128]{2,1,0:T(8,128)S(1)}, u32[]{:S(2)}, u32[]{:S(2)}) collective-permute-start(f32[6,48,128]{2,1,0:T(8,128)S(1)} %get-tuple-element.49), channel_id=1, source_target_pairs={{0,1},{1,0},{2,3},{3,2},{4,5},{5,4},{6,7},{7,6},{8,9},{9,8},{10,11... | collective-permute-start | bytes 442376 | tf_op jit(solution)/shard_map/ppermute | solution.py:575
  4.5 24.1 %collective-permute-start.1 = (f32[6,48,128]{2,1,0:T(8,128)S(1)}, f32[6,48,128]{2,1,0:T(8,128)S(1)}, u32[]{:S(2)}, u32[]{:S(2)}) collective-permute-start(f32[6,48,128]{2,1,0:T(8,128)S(1)} %get-tuple-element.50), channel_id=1, source_target_pairs={{0,32},{1,33},{2,34},{3,35},{4,36},{5,37},{6,38},{7,39},{8,40},{9,... | collective-permute-start | bytes 442376 | tf_op jit(solution)/shard_map/ppermute | solution.py:575
  6.4 22.2 %collective-permute-start.2 = (f32[6,48,128]{2,1,0:T(8,128)S(1)}, f32[6,48,128]{2,1,0:T(8,128)S(1)}, u32[]{:S(2)}, u32[]{:S(2)}) collective-permute-start(f32[6,48,128]{2,1,0:T(8,128)S(1)} %get-tuple-element.51), channel_id=1, source_target_pairs={{0,32},{1,2},{2,1},{3,4},{4,3},{5,6},{6,5},{7,8},{8,7},{9,10},{10,... | collective-permute-start | bytes 442376 | tf_op jit(solution)/shard_map/ppermute | solution.py:575
  6.4 22.2 %collective-permute-start.3 = (f32[6,48,128]{2,1,0:T(8,128)S(1)}, f32[6,48,128]{2,1,0:T(8,128)S(1)}, u32[]{:S(2)}, u32[]{:S(2)}) collective-permute-start(f32[6,48,128]{2,1,0:T(8,128)S(1)} %get-tuple-element.52), channel_id=1, source_target_pairs={{0,1},{1,0},{2,3},{3,2},{4,5},{5,4},{6,7},{7,6},{8,9},{9,8},{10,11... | collective-permute-start | bytes 442376 | tf_op jit(solution)/shard_map/ppermute | solution.py:575
  15.4 24.7 %all-to-all-start = ((f32[256,1,128]{2,1,0:T(1,128)}), f32[256,1,128]{2,1,0:T(1,128)S(1)}, u32[]{:S(2)}, u32[]{:S(2)}) async-start(f32[256,1,128]{2,1,0:T(1,128)} %bitcast.3), calls=%async_computation | async-start | bytes 262144 | tf_op jit(solution)/shard_map/all_to_all | solution.py:627
  28.6 11.5 %copy-start = (f32[8192]{0:T(1024)S(1)}, f32[8192]{0:T(1024)}, u32[]{:S(2)}) copy-start(f32[8192]{0:T(1024)} %param.8) | copy-start | bytes 98308
  41.1 3.4 %collective-permute-start.7 = (f32[3,48,128]{2,1,0:T(8,128)S(1)}, f32[3,48,128]{2,1,0:T(8,128)S(1)}, u32[]{:S(2)}, u32[]{:S(2)}) collective-permute-start(f32[3,48,128]{2,1,0:T(8,128)S(1)} %get-tuple-element.60), channel_id=1, source_target_pairs={{0,1},{1,0},{2,3},{3,2},{4,5},{5,4},{6,7},{7,6},{8,9},{9,8},{10,11... | collective-permute-start | bytes 221192 | tf_op jit(solution)/shard_map/ppermute | solution.py:575
  42.3 6.8 %collective-permute-start.4 = (f32[3,48,128]{2,1,0:T(8,128)S(1)}, f32[3,48,128]{2,1,0:T(8,128)S(1)}, u32[]{:S(2)}, u32[]{:S(2)}) collective-permute-start(f32[3,48,128]{2,1,0:T(8,128)S(1)} %get-tuple-element.56), channel_id=1, source_target_pairs={{0,32},{1,33},{2,34},{3,35},{4,36},{5,37},{6,38},{7,39},{8,40},{9,... | collective-permute-start | bytes 221192 | tf_op jit(solution)/shard_map/ppermute | solution.py:575
  43.4 5.7 %collective-permute-start.5 = (f32[3,48,128]{2,1,0:T(8,128)S(1)}, f32[3,48,128]{2,1,0:T(8,128)S(1)}, u32[]{:S(2)}, u32[]{:S(2)}) collective-permute-start(f32[3,48,128]{2,1,0:T(8,128)S(1)} %get-tuple-element.57), channel_id=1, source_target_pairs={{0,32},{1,2},{2,1},{3,4},{4,3},{5,6},{6,5},{7,8},{8,7},{9,10},{10,... | collective-permute-start | bytes 221192 | tf_op jit(solution)/shard_map/ppermute | solution.py:575
  44.0 5.2 %collective-permute-start.6 = (f32[3,48,128]{2,1,0:T(8,128)S(1)}, f32[3,48,128]{2,1,0:T(8,128)S(1)}, u32[]{:S(2)}, u32[]{:S(2)}) collective-permute-start(f32[3,48,128]{2,1,0:T(8,128)S(1)} %get-tuple-element.58), channel_id=1, source_target_pairs={{0,1},{1,0},{2,3},{3,2},{4,5},{5,4},{6,7},{7,6},{8,9},{9,8},{10,11... | collective-permute-start | bytes 221192 | tf_op jit(solution)/shard_map/ppermute | solution.py:575
  57.0 4.7 %collective-permute-start.11 = (f32[3,48,128]{2,1,0:T(8,128)S(1)}, f32[3,48,128]{2,1,0:T(8,128)S(1)}, u32[]{:S(2)}, u32[]{:S(2)}) collective-permute-start(f32[3,48,128]{2,1,0:T(8,128)S(1)} %get-tuple-element.68), channel_id=1, source_target_pairs={{0,1},{1,0},{2,3},{3,2},{4,5},{5,4},{6,7},{7,6},{8,9},{9,8},{10,11... | collective-permute-start | bytes 221192 | tf_op jit(solution)/shard_map/ppermute | solution.py:575
  57.1 9.3 %collective-permute-start.8 = (f32[3,48,128]{2,1,0:T(8,128)S(1)}, f32[3,48,128]{2,1,0:T(8,128)S(1)}, u32[]{:S(2)}, u32[]{:S(2)}) collective-permute-start(f32[3,48,128]{2,1,0:T(8,128)S(1)} %get-tuple-element.65), channel_id=1, source_target_pairs={{0,32},{1,33},{2,34},{3,35},{4,36},{5,37},{6,38},{7,39},{8,40},{9,... | collective-permute-start | bytes 221192 | tf_op jit(solution)/shard_map/ppermute | solution.py:575
  57.2 9.2 %collective-permute-start.9 = (f32[3,48,128]{2,1,0:T(8,128)S(1)}, f32[3,48,128]{2,1,0:T(8,128)S(1)}, u32[]{:S(2)}, u32[]{:S(2)}) collective-permute-start(f32[3,48,128]{2,1,0:T(8,128)S(1)} %get-tuple-element.66), channel_id=1, source_target_pairs={{0,32},{1,2},{2,1},{3,4},{4,3},{5,6},{6,5},{7,8},{8,7},{9,10},{10,... | collective-permute-start | bytes 221192 | tf_op jit(solution)/shard_map/ppermute | solution.py:575
  60.2 6.2 %collective-permute-start.10 = (f32[3,48,128]{2,1,0:T(8,128)S(1)}, f32[3,48,128]{2,1,0:T(8,128)S(1)}, u32[]{:S(2)}, u32[]{:S(2)}) collective-permute-start(f32[3,48,128]{2,1,0:T(8,128)S(1)} %get-tuple-element.67), channel_id=1, source_target_pairs={{0,1},{1,0},{2,3},{3,2},{4,5},{5,4},{6,7},{7,6},{8,9},{9,8},{10,11... | collective-permute-start | bytes 221192 | tf_op jit(solution)/shard_map/ppermute | solution.py:575
  74.1 4.5 %collective-permute-start.15 = (f32[3,48,128]{2,1,0:T(8,128)S(1)}, f32[3,48,128]{2,1,0:T(8,128)S(1)}, u32[]{:S(2)}, u32[]{:S(2)}) collective-permute-start(f32[3,48,128]{2,1,0:T(8,128)S(1)} %get-tuple-element.76), channel_id=1, source_target_pairs={{0,1},{1,0},{2,3},{3,2},{4,5},{5,4},{6,7},{7,6},{8,9},{9,8},{10,11... | collective-permute-start | bytes 221192 | tf_op jit(solution)/shard_map/ppermute | solution.py:575
  74.2 9.1 %collective-permute-start.12 = (f32[3,48,128]{2,1,0:T(8,128)S(1)}, f32[3,48,128]{2,1,0:T(8,128)S(1)}, u32[]{:S(2)}, u32[]{:S(2)}) collective-permute-start(f32[3,48,128]{2,1,0:T(8,128)S(1)} %get-tuple-element.73), channel_id=1, source_target_pairs={{0,32},{1,33},{2,34},{3,35},{4,36},{5,37},{6,38},{7,39},{8,40},{9,... | collective-permute-start | bytes 221192 | tf_op jit(solution)/shard_map/ppermute | solution.py:575
  74.3 9.0 %collective-permute-start.13 = (f32[3,48,128]{2,1,0:T(8,128)S(1)}, f32[3,48,128]{2,1,0:T(8,128)S(1)}, u32[]{:S(2)}, u32[]{:S(2)}) collective-permute-start(f32[3,48,128]{2,1,0:T(8,128)S(1)} %get-tuple-element.74), channel_id=1, source_target_pairs={{0,32},{1,2},{2,1},{3,4},{4,3},{5,6},{6,5},{7,8},{8,7},{9,10},{10,... | collective-permute-start | bytes 221192 | tf_op jit(solution)/shard_map/ppermute | solution.py:575
  77.3 6.0 %collective-permute-start.14 = (f32[3,48,128]{2,1,0:T(8,128)S(1)}, f32[3,48,128]{2,1,0:T(8,128)S(1)}, u32[]{:S(2)}, u32[]{:S(2)}) collective-permute-start(f32[3,48,128]{2,1,0:T(8,128)S(1)} %get-tuple-element.75), channel_id=1, source_target_pairs={{0,1},{1,0},{2,3},{3,2},{4,5},{5,4},{6,7},{7,6},{8,9},{9,8},{10,11... | collective-permute-start | bytes 221192 | tf_op jit(solution)/shard_map/ppermute | solution.py:575
  91.8 3.3 %collective-permute-start.19 = (f32[3,48,128]{2,1,0:T(8,128)S(1)}, f32[3,48,128]{2,1,0:T(8,128)S(1)}, u32[]{:S(2)}, u32[]{:S(2)}) collective-permute-start(f32[3,48,128]{2,1,0:T(8,128)S(1)} %get-tuple-element.85), channel_id=1, source_target_pairs={{0,1},{1,0},{2,3},{3,2},{4,5},{5,4},{6,7},{7,6},{8,9},{9,8},{10,11... | collective-permute-start | bytes 221192 | tf_op jit(solution)/shard_map/ppermute | solution.py:575
  91.9 7.8 %collective-permute-start.16 = (f32[3,48,128]{2,1,0:T(8,128)S(1)}, f32[3,48,128]{2,1,0:T(8,128)S(1)}, u32[]{:S(2)}, u32[]{:S(2)}) collective-permute-start(f32[3,48,128]{2,1,0:T(8,128)S(1)} %get-tuple-element.82), channel_id=1, source_target_pairs={{0,32},{1,33},{2,34},{3,35},{4,36},{5,37},{6,38},{7,39},{8,40},{9,... | collective-permute-start | bytes 221192 | tf_op jit(solution)/shard_map/ppermute | solution.py:575
  92.0 7.7 %collective-permute-start.17 = (f32[3,48,128]{2,1,0:T(8,128)S(1)}, f32[3,48,128]{2,1,0:T(8,128)S(1)}, u32[]{:S(2)}, u32[]{:S(2)}) collective-permute-start(f32[3,48,128]{2,1,0:T(8,128)S(1)} %get-tuple-element.83), channel_id=1, source_target_pairs={{0,32},{1,2},{2,1},{3,4},{4,3},{5,6},{6,5},{7,8},{8,7},{9,10},{10,... | collective-permute-start | bytes 221192 | tf_op jit(solution)/shard_map/ppermute | solution.py:575
  93.3 6.4 %collective-permute-start.18 = (f32[3,48,128]{2,1,0:T(8,128)S(1)}, f32[3,48,128]{2,1,0:T(8,128)S(1)}, u32[]{:S(2)}, u32[]{:S(2)}) collective-permute-start(f32[3,48,128]{2,1,0:T(8,128)S(1)} %get-tuple-element.84), channel_id=1, source_target_pairs={{0,1},{1,0},{2,3},{3,2},{4,5},{5,4},{6,7},{7,6},{8,9},{9,8},{10,11... | collective-permute-start | bytes 221192 | tf_op jit(solution)/shard_map/ppermute | solution.py:575

commit v2 on v1

--- a/solution.py
+++ b/solution.py
@@ -50,8 +50,20 @@
     return high, mid, round_bf16(rest - mid)
 
 
+def slab_index():
+    return lax.axis_index("slab")
+
+
+def cell_index():
+    return 2 * lax.axis_index("chip") + lax.axis_index("core")
+
+
+def n_slabs_cells():
+    return lax.axis_size("slab"), 2 * lax.axis_size("chip")
+
+
 def parity():
-    return lax.axis_index("slab") % 2, lax.axis_index("cell") % 2
+    return slab_index() % 2, cell_index() % 2
 
 
 def send_rows():
@@ -78,10 +90,9 @@
 
 def slot_exists():
     out = []
-    for axis in ("slab", "cell"):
-        i = lax.axis_index(axis)
+    for i, n in zip((slab_index(), cell_index()), n_slabs_cells()):
         partner = i - 1 + 2 * (i % 2)
-        out.append((partner >= 0) & (partner < lax.axis_size(axis)))
+        out.append((partner >= 0) & (partner < n))
     return None, out[0], out[1], None
 
 
@@ -105,9 +116,7 @@
 
 
 def centre_of():
-    slab = lax.axis_index("slab").astype(f32)
-    cell = lax.axis_index("cell").astype(f32)
-    return slab, cell
+    return slab_index().astype(f32), cell_index().astype(f32)
 
 
 def list_pairs(near_list, near_count):
@@ -201,8 +210,8 @@
 
 
 def far_kernel(
-    scalars_in, places, burgers, out, control_out, acc, rows, cols, apart_by, w_even, w_odd,
-    scalars, control, sems
+    scalars_in, places, burgers, mine_out, other_out, control_out, acc, rows, cols, apart_by, w_even, w_odd,
+    scalars, control, sems, by_target
 ):
     copy = pltpu.make_async_copy(scalars_in, scalars, sems.at[0])
     copy.start()
@@ -302,7 +311,11 @@
             gradient.append(-3.0 * (apart[k] * total[a] - moment))
     zero = jnp.zeros((LANES - 12, 2 * LANES), f32)
     values = jnp.concatenate(direct + gradient + [zero], axis=0)
-    out[...] = jnp.concatenate([values[:, :LANES].T, values[:, LANES:].T], axis=0)
+    by_target[...] = jnp.concatenate([values[:, :LANES].T, values[:, LANES:].T], axis=0)
+    first, second = (by_target[pl.ds(i, LANES, stride=2), :] for i in range(2))
+    here = lax.axis_index("core") == 0
+    mine_out[...] = jnp.where(here, first, second)
+    other_out[...] = jnp.where(here, second, first)
     copy.wait()
 
 
@@ -557,7 +570,7 @@
 
 
 def swap(x, slot):
-    n_slabs, n_cells = lax.axis_size("slab"), lax.axis_size("cell")
+    n_slabs, n_cells = n_slabs_cells()
     pairs = []
     for s in range(n_slabs):
         for c in range(n_cells):
@@ -572,7 +585,7 @@
                 t = c - 1 + 2 * (c % 2)
                 to = (s, t) if 0 <= t < n_cells else (s ^ 1, c)
             pairs.append((s * n_cells + c, to[0] * n_cells + to[1]))
-    return lax.ppermute(x, ("slab", "cell"), pairs)
+    return lax.ppermute(x, ("slab", "chip", "core"), pairs)
 
 
 def exchange(sends):
@@ -604,11 +617,11 @@
     )(numbers, positions, burgers)
     ghosts = [swap(x, slot) for x, slot in zip(sends, (3, 0, 2, 1))]
 
-    shares, control = pl.pallas_call(
+    mine, other, control = pl.pallas_call(
         far_kernel,
-        out_shape=[shape(EXT, LANES), shape(CONTROL, dtype=jnp.int32)],
+        out_shape=[shape(EXT // 2, LANES)] * 2 + [shape(CONTROL, dtype=jnp.int32)],
         in_specs=[vmem] * 3,
-        out_specs=[vmem] * 2,
+        out_specs=[vmem] * 3,
         scratch_shapes=[
             pltpu.VMEM((32, 2 * EXT), f32),
             pltpu.VMEM((BLOCKS // 4, LANES, LANES), f32),
@@ -619,12 +632,13 @@
             pltpu.SMEM((16, LANES), jnp.int32),
             pltpu.SMEM((CONTROL,), jnp.int32),
             pltpu.SemaphoreType.DMA((2,)),
+            pltpu.VMEM((EXT, LANES), f32),
         ],
         compiler_params=params,
         cost_estimate=cost(20e9),
         name="far",
     )(scalars, places, burgers)
-    shares = lax.all_to_all(shares, ("slab", "cell"), 0, 0, tiled=True)
+    shares = lax.all_to_all(mine + swap(other, 3), ("slab", "chip"), 0, 0, tiled=True)
 
     near, burg = pl.pallas_call(
         first_kernel,
@@ -684,18 +698,22 @@
     return moved, velocity
 
 
+AXES = ("slab", "chip", "core")
+
+
 def solution(mesh):
+    n_slabs, n_cells = mesh.devices.shape
     return jax.shard_map(
         local,
-        mesh=mesh,
+        mesh=jax.sharding.Mesh(mesh.devices.reshape(n_slabs, n_cells // 2, 2), AXES),
         in_specs=(
-            P(None, ("slab", "cell")),
-            P(None, ("slab", "cell")),
-            P(("slab", "cell")),
-            P(("slab", "cell"), None),
-            P(("slab", "cell")),
-            P(None, ("slab", "cell")),
+            P(None, AXES),
+            P(None, AXES),
+            P(AXES),
+            P(AXES, None),
+            P(AXES),
+            P(None, AXES),
         ),
-        out_specs=(P(None, ("slab", "cell")), P(None, ("slab", "cell"))),
+        out_specs=(P(None, AXES), P(None, AXES)),
         check_vma=False,
     )

time: 107 us -> 110 us (1.028)
  the two profiles are of different devices: /device:TPU:9 before, /device:TPU:103 now
where the time goes in v2:
time: 110 us
  Pallas kernels  70.9 us (64%)
  starting transfers between devices  32.9 us (30%)
  waiting for transfers between devices  2.33 us (2%)
  other arithmetic  1.37 us (1%)
  between operations  1.13 us (1%)
    pallas_call x4, Pallas kernels, evaluate(): pl.pallas_call(kernel, out_shape=out_shape, in_specs=[vmem] * (7 + len(LA...  26.6 us
    ppermute x21, starting transfers between devices, swap(): return lax.ppermute(x, ('slab', 'chip', 'core'), pairs)  23.8 us
    pallas_call x4, Pallas kernels, evaluate(): pl.pallas_call(early_kernel, out_shape=[shape(*right_shape, dtype=bf16),...  23.7 us
    pallas_call x1, Pallas kernels, local(): pl.pallas_call(first_kernel, out_shape=[block, shape((EXT + 1) * 8, LANES...  11.4 us
    all_to_all x1, starting transfers between devices, local(): lax.all_to_all(mine + swap(other, 3), ('slab', 'chip'), 0, 0, tiled=True)  9.04 us
    pallas_call x1, Pallas kernels, local(): pl.pallas_call(far_kernel, out_shape=[shape(EXT // 2, LANES)] * 2 + [shap...  6.88 us
    ppermute x21, waiting for transfers between devices, swap(): return lax.ppermute(x, ('slab', 'chip', 'core'), pairs)  2.33 us
  transfers between devices with their start and end apart: 22, of which 3 were waited for; matrix products, arithmetic and copies ran while one was open for 1% of the time, Pallas kernels for 38%

profile of v2, /device:TPU:103, one launch (start us, length us, event | category | flops | bytes accessed | tf_op | source)
XLA Modules:
  0.0 109.6 jit_solution(10175998900264476579)
XLA Ops:
  0.6 1.0 copy_bitcast_fusion
  2.3 1.4 %pack.1 = (f32[3,64,128]{2,1,0:T(8,128)S(1)}, s32[16,128]{1,0:T(8,128)S(1)}, f32[6,48,128]{2,1,0:T(8,128)S(1)}, f32[6,48,128]{2,1,0:T(8,128)S(1)}, f32[6,48,128]{2,1,0:T(8,128)S(1)}, /*index=5*/f32[6,48,128]{2,1,0:T(8,128)S(1)}) custom-call(s32[16,128]{1,0:T(8,128)S(1)} %pad_add_fusion.numbers, f32[3,64,128]{2,1,0:T(8,128)S(1)} %get-tuple-element.91.positions, ...), custom_call_target="tpu_custom_call" | custom-call | tf_op jit(solution)/shard_map/pack/pallas_call | solution.py:609
  4.5 1.3 %collective-permute-start.2 = (f32[6,48,128]{2,1,0:T(8,128)S(1)}, f32[6,48,128]{2,1,0:T(8,128)S(1)}, u32[]{:S(2)}, u32[]{:S(2)}) collective-permute-start(f32[6,48,128]{2,1,0:T(8,128)S(1)} %get-tuple-element.52), channel_id=1, source_target_pairs={{0,32},{1,33},{2,34},{3,35},{4,36},{5,37},{6,38},{7,39},{8,40},{9,... | collective-permute-start | bytes 442376 | tf_op jit(solution)/shard_map/ppermute | solution.py:588
  5.8 3.4 %collective-permute-start.3 = (f32[6,48,128]{2,1,0:T(8,128)S(1)}, f32[6,48,128]{2,1,0:T(8,128)S(1)}, u32[]{:S(2)}, u32[]{:S(2)}) collective-permute-start(f32[6,48,128]{2,1,0:T(8,128)S(1)} %get-tuple-element.53), channel_id=1, source_target_pairs={{0,32},{1,2},{2,1},{3,4},{4,3},{5,6},{6,5},{7,8},{8,7},{9,10},{10,... | collective-permute-start | bytes 442376 | tf_op jit(solution)/shard_map/ppermute | solution.py:588
  9.2 2.4 %collective-permute-start.4 = (f32[6,48,128]{2,1,0:T(8,128)S(1)}, f32[6,48,128]{2,1,0:T(8,128)S(1)}, u32[]{:S(2)}, u32[]{:S(2)}) collective-permute-start(f32[6,48,128]{2,1,0:T(8,128)S(1)} %get-tuple-element.54), channel_id=1, source_target_pairs={{0,1},{1,0},{2,3},{3,2},{4,5},{5,4},{6,7},{7,6},{8,9},{9,8},{10,11... | collective-permute-start | bytes 442376 | tf_op jit(solution)/shard_map/ppermute | solution.py:588
  11.6 6.9 %far.1 = (f32[128,128]{1,0:T(8,128)S(1)}, f32[128,128]{1,0:T(8,128)S(1)}, s32[1112]{0:T(1024)S(1)}) custom-call(s32[16,128]{1,0:T(8,128)S(1)} %get-tuple-element.46.scalars_in, f32[3,64,128]{2,1,0:T(8,128)S(1)} %get-tuple-element.47.places.own, f32[3,64,128]{2,1,0:T(8,128)S(1)} %get-tuple-element.90.burgers), custom_call_target="tpu_custom_call" | custom-call | flops 20000000000 | bytes 1048576 | tf_op jit(solution)/shard_map/far/pallas_call | solution.py:620
  18.6 1.2 %collective-permute-done = f32[128,128]{1,0:T(8,128)S(1)} collective-permute-done((f32[128,128]{1,0:T(8,128)S(1)}, f32[128,128]{1,0:T(8,128)S(1)}, u32[]{:S(2)}, u32[]{:S(2)}) %collective-permute-start) | collective-permute-done | bytes 65568 | tf_op jit(solution)/shard_map/ppermute | solution.py:588
  20.5 9.0 %all-to-all-start = ((f32[128,1,128]{2,1,0:T(1,128)}), f32[128,1,128]{2,1,0:T(1,128)S(1)}, u32[]{:S(2)}, u32[]{:S(2)}) async-start(f32[128,1,128]{2,1,0:T(1,128)} %bitcast.3), calls=%async_computation | async-start | bytes 131072 | tf_op jit(solution)/shard_map/all_to_all | solution.py:641
  29.6 11.4 %near_first.1 = (f32[3,64,128]{2,1,0:T(8,128)S(1)}, f32[2056,128]{1,0:T(8,128)S(1)}) custom-call(s32[1112]{0:T(1024)S(1)} %get-tuple-element.48.control_in.control, f32[3,64,128]{2,1,0:T(8,128)S(1)} %get-tuple-element.47.places.own, f32[3,64,128]{2,1,0:T(8,128)S(1)} %get-tuple-element.90.burgers, f32[6,48,128]{2,1,0:T(8,128)S(1)} %collective-permute-done.1.g3, ...), custom_call_target="tpu_custom_call" | custom-call | flops 20000000000 | bytes 1048576 | tf_op jit(solution)/shard_map/near_first/pallas_call | solution.py:643
  41.0 1.0 start.1
  42.1 1.6 %collective-permute-start.5 = (f32[3,48,128]{2,1,0:T(8,128)S(1)}, f32[3,48,128]{2,1,0:T(8,128)S(1)}, u32[]{:S(2)}, u32[]{:S(2)}) collective-permute-start(f32[3,48,128]{2,1,0:T(8,128)S(1)} %get-tuple-element.58), channel_id=1, source_target_pairs={{0,32},{1,33},{2,34},{3,35},{4,36},{5,37},{6,38},{7,39},{8,40},{9,... | collective-permute-start | bytes 221192 | tf_op jit(solution)/shard_map/ppermute | solution.py:588
  43.7 5.0 %collective-permute-start.7 = (f32[3,48,128]{2,1,0:T(8,128)S(1)}, f32[3,48,128]{2,1,0:T(8,128)S(1)}, u32[]{:S(2)}, u32[]{:S(2)}) collective-permute-start(f32[3,48,128]{2,1,0:T(8,128)S(1)} %get-tuple-element.60), channel_id=1, source_target_pairs={{0,1},{1,0},{2,3},{3,2},{4,5},{5,4},{6,7},{7,6},{8,9},{9,8},{10,11... | collective-permute-start | bytes 221192 | tf_op jit(solution)/shard_map/ppermute | solution.py:588
  48.7 6.1 %near_early.4 = (bf16[64,8,16,128]{3,2,1,0:T(8,128)(2,1)S(1)}, f32[512,128]{1,0:T(8,128)S(1)}) custom-call(s32[1112]{0:T(1024)S(1)} %get-tuple-element.48.control_in.control, f32[3,64,128]{2,1,0:T(8,128)S(1)} %get-tuple-element.57.own, f32[3,48,128]{2,1,0:T(8,128)S(1)} %collective-permute-done.8.g3, f32[2056,128]{1,0:T(8,128)S(1)} %get-tuple-element.61.burg), custom_call_target="tpu_custom_call" | custom-call | flops 20000000000 | bytes 1048576 | tf_op jit(solution)/shard_map/near_early/pallas_call | solution.py:667
  54.8 6.4 %near_step.3 = (f32[3,64,128]{2,1,0:T(8,128)S(1)}, f32[3,64,128]{2,1,0:T(8,128)S(1)}, f32[3,48,128]{2,1,0:T(8,128)S(1)}, f32[3,48,128]{2,1,0:T(8,128)S(1)}, f32[...) custom-call(s32[1112]{0:T(1024)S(1)} %get-tuple-element.48.control_in.control, ...), custom_call_target="tpu_custom_call" | custom-call | flops 10000000000 | bytes 1048576 | tf_op jit(solution)/shard_map/near_step/pallas_call | solution.py:677
  61.5 1.1 %collective-permute-start.11 = (f32[3,48,128]{2,1,0:T(8,128)S(1)}, f32[3,48,128]{2,1,0:T(8,128)S(1)}, u32[]{:S(2)}, u32[]{:S(2)}) collective-permute-start(f32[3,48,128]{2,1,0:T(8,128)S(1)} %get-tuple-element.69), channel_id=1, source_target_pairs={{0,1},{1,0},{2,3},{3,2},{4,5},{5,4},{6,7},{7,6},{8,9},{9,8},{10,11... | collective-permute-start | bytes 221192 | tf_op jit(solution)/shard_map/ppermute | solution.py:588
  62.6 5.9 %near_early.5 = (bf16[64,8,16,128]{3,2,1,0:T(8,128)(2,1)S(1)}, f32[512,128]{1,0:T(8,128)S(1)}) custom-call(s32[1112]{0:T(1024)S(1)} %get-tuple-element.48.control_in.control, f32[3,64,128]{2,1,0:T(8,128)S(1)} %get-tuple-element.66.own, f32[3,48,128]{2,1,0:T(8,128)S(1)} %collective-permute-done.12.g3, f32[2056,128]{1,0:T(8,128)S(1)} %get-tuple-element.61.burg), custom_call_target="tpu_custom_call" | custom-call | flops 20000000000 | bytes 1048576 | tf_op jit(solution)/shard_map/near_early/pallas_call | solution.py:667
  68.9 6.4 %near_step.4 = (f32[3,64,128]{2,1,0:T(8,128)S(1)}, f32[3,64,128]{2,1,0:T(8,128)S(1)}, f32[3,48,128]{2,1,0:T(8,128)S(1)}, f32[3,48,128]{2,1,0:T(8,128)S(1)}, f32[...) custom-call(s32[1112]{0:T(1024)S(1)} %get-tuple-element.48.control_in.control, ...), custom_call_target="tpu_custom_call" | custom-call | flops 10000000000 | bytes 1048576 | tf_op jit(solution)/shard_map/near_step/pallas_call | solution.py:677
  75.5 2.0 %collective-permute-start.14 = (f32[3,48,128]{2,1,0:T(8,128)S(1)}, f32[3,48,128]{2,1,0:T(8,128)S(1)}, u32[]{:S(2)}, u32[]{:S(2)}) collective-permute-start(f32[3,48,128]{2,1,0:T(8,128)S(1)} %get-tuple-element.76), channel_id=1, source_target_pairs={{0,32},{1,2},{2,1},{3,4},{4,3},{5,6},{6,5},{7,8},{8,7},{9,10},{10,... | collective-permute-start | bytes 221192 | tf_op jit(solution)/shard_map/ppermute | solution.py:588
  77.5 1.4 %collective-permute-start.15 = (f32[3,48,128]{2,1,0:T(8,128)S(1)}, f32[3,48,128]{2,1,0:T(8,128)S(1)}, u32[]{:S(2)}, u32[]{:S(2)}) collective-permute-start(f32[3,48,128]{2,1,0:T(8,128)S(1)} %get-tuple-element.77), channel_id=1, source_target_pairs={{0,1},{1,0},{2,3},{3,2},{4,5},{5,4},{6,7},{7,6},{8,9},{9,8},{10,11... | collective-permute-start | bytes 221192 | tf_op jit(solution)/shard_map/ppermute | solution.py:588
  78.9 5.9 %near_early.6 = (bf16[64,8,16,128]{3,2,1,0:T(8,128)(2,1)S(1)}, f32[512,128]{1,0:T(8,128)S(1)}) custom-call(s32[1112]{0:T(1024)S(1)} %get-tuple-element.48.control_in.control, f32[3,64,128]{2,1,0:T(8,128)S(1)} %get-tuple-element.74.own, f32[3,48,128]{2,1,0:T(8,128)S(1)} %collective-permute-done.16.g3, f32[2056,128]{1,0:T(8,128)S(1)} %get-tuple-element.61.burg), custom_call_target="tpu_custom_call" | custom-call | flops 20000000000 | bytes 1048576 | tf_op jit(solution)/shard_map/near_early/pallas_call | solution.py:667
  85.6 7.2 %near_step.5 = (f32[3,8192]{1,0:T(4,128)}, f32[3,64,128]{2,1,0:T(8,128)S(1)}, f32[3,48,128]{2,1,0:T(8,128)S(1)}, f32[3,48,128]{2,1,0:T(8,128)S(1)}, f32[3,48,128...) custom-call(s32[1112]{0:T(1024)S(1)} %get-tuple-element.48.control_in.control, f32[8,128]{1,0:T(8,128)S(1)} %get-tuple-element.56.expansion, ...), custom_call_target="tpu_custom_call" | custom-call | flops 10000000000 | bytes 1048576 | tf_op jit(solution)/shard_map/near_step/pallas_call | solution.py:677
  93.3 3.6 %collective-permute-start.19 = (f32[3,48,128]{2,1,0:T(8,128)S(1)}, f32[3,48,128]{2,1,0:T(8,128)S(1)}, u32[]{:S(2)}, u32[]{:S(2)}) collective-permute-start(f32[3,48,128]{2,1,0:T(8,128)S(1)} %get-tuple-element.86), channel_id=1, source_target_pairs={{0,1},{1,0},{2,3},{3,2},{4,5},{5,4},{6,7},{7,6},{8,9},{9,8},{10,11... | collective-permute-start | bytes 221192 | tf_op jit(solution)/shard_map/ppermute | solution.py:588
  97.0 5.8 %near_early.7 = (bf16[64,8,16,128]{3,2,1,0:T(8,128)(2,1)S(1)}, f32[512,128]{1,0:T(8,128)S(1)}) custom-call(s32[1112]{0:T(1024)S(1)} %get-tuple-element.48.control_in.control, f32[3,64,128]{2,1,0:T(8,128)S(1)} %get-tuple-element.83.own, f32[3,48,128]{2,1,0:T(8,128)S(1)} %collective-permute-done.20.g3, f32[2056,128]{1,0:T(8,128)S(1)} %get-tuple-element.61.burg), custom_call_target="tpu_custom_call" | custom-call | flops 20000000000 | bytes 1048576 | tf_op jit(solution)/shard_map/near_early/pallas_call | solution.py:667
  102.8 6.6 %near_last.1 = f32[3,8192]{1,0:T(4,128)} custom-call(s32[1112]{0:T(1024)S(1)} %get-tuple-element.48.control_in.control, f32[8,128]{1,0:T(8,128)S(1)} %get-tuple-element.56.expansion, f32[3,64,128]{2,1,0:T(8,128)S(1)} %get-tuple-element.83.own, f32[3,48,128]{2,1,0:T(8,128)S(1)} %collective-permute-done.17.g0, f32[3,48,128]{2,1,0:T(8,128)S(1)} %collective-permute-done.18.g2, ...), custom_call_target="tpu_custom_call" | custom-call | flops 10000000000 | bytes 1048576 | tf_op jit(solution)/shard_map/near_last/pallas_call | solution.py:677
  (37 shorter events, 4.4 us)
Async XLA Ops:
  3.7 25.8 %collective-permute-start.1 = (f32[6,48,128]{2,1,0:T(8,128)S(1)}, f32[6,48,128]{2,1,0:T(8,128)S(1)}, u32[]{:S(2)}, u32[]{:S(2)}) collective-permute-start(f32[6,48,128]{2,1,0:T(8,128)S(1)} %get-tuple-element.51), channel_id=1, source_target_pairs={{0,1},{1,0},{2,3},{3,2},{4,5},{5,4},{6,7},{7,6},{8,9},{9,8},{10,11... | collective-permute-start | bytes 442376 | tf_op jit(solution)/shard_map/ppermute | solution.py:588
  4.5 25.1 %collective-permute-start.2 = (f32[6,48,128]{2,1,0:T(8,128)S(1)}, f32[6,48,128]{2,1,0:T(8,128)S(1)}, u32[]{:S(2)}, u32[]{:S(2)}) collective-permute-start(f32[6,48,128]{2,1,0:T(8,128)S(1)} %get-tuple-element.52), channel_id=1, source_target_pairs={{0,32},{1,33},{2,34},{3,35},{4,36},{5,37},{6,38},{7,39},{8,40},{9,... | collective-permute-start | bytes 442376 | tf_op jit(solution)/shard_map/ppermute | solution.py:588
  5.8 23.8 %collective-permute-start.3 = (f32[6,48,128]{2,1,0:T(8,128)S(1)}, f32[6,48,128]{2,1,0:T(8,128)S(1)}, u32[]{:S(2)}, u32[]{:S(2)}) collective-permute-start(f32[6,48,128]{2,1,0:T(8,128)S(1)} %get-tuple-element.53), channel_id=1, source_target_pairs={{0,32},{1,2},{2,1},{3,4},{4,3},{5,6},{6,5},{7,8},{8,7},{9,10},{10,... | collective-permute-start | bytes 442376 | tf_op jit(solution)/shard_map/ppermute | solution.py:588
  9.2 20.4 %collective-permute-start.4 = (f32[6,48,128]{2,1,0:T(8,128)S(1)}, f32[6,48,128]{2,1,0:T(8,128)S(1)}, u32[]{:S(2)}, u32[]{:S(2)}) collective-permute-start(f32[6,48,128]{2,1,0:T(8,128)S(1)} %get-tuple-element.54), channel_id=1, source_target_pairs={{0,1},{1,0},{2,3},{3,2},{4,5},{5,4},{6,7},{7,6},{8,9},{9,8},{10,11... | collective-permute-start | bytes 442376 | tf_op jit(solution)/shard_map/ppermute | solution.py:588
  18.5 1.3 %collective-permute-start = (f32[128,128]{1,0:T(8,128)S(1)}, f32[128,128]{1,0:T(8,128)S(1)}, u32[]{:S(2)}, u32[]{:S(2)}) collective-permute-start(f32[128,128]{1,0:T(8,128)S(1)} %get-tuple-element.50), channel_id=1, source_target_pairs={{0,1},{1,0},{2,3},{3,2},{4,5},{5,4},{6,7},{7,6},{8,9},{9,8},{10,11... | collective-permute-start | bytes 196616 | tf_op jit(solution)/shard_map/ppermute | solution.py:588
  20.5 20.5 %all-to-all-start = ((f32[128,1,128]{2,1,0:T(1,128)}), f32[128,1,128]{2,1,0:T(1,128)S(1)}, u32[]{:S(2)}, u32[]{:S(2)}) async-start(f32[128,1,128]{2,1,0:T(1,128)} %bitcast.3), calls=%async_computation | async-start | bytes 131072 | tf_op jit(solution)/shard_map/all_to_all | solution.py:641
  29.6 11.4 %copy-start = (f32[8192]{0:T(1024)S(1)}, f32[8192]{0:T(1024)}, u32[]{:S(2)}) copy-start(f32[8192]{0:T(1024)} %param.8) | copy-start | bytes 98308
  42.0 6.7 %collective-permute-start.8 = (f32[3,48,128]{2,1,0:T(8,128)S(1)}, f32[3,48,128]{2,1,0:T(8,128)S(1)}, u32[]{:S(2)}, u32[]{:S(2)}) collective-permute-start(f32[3,48,128]{2,1,0:T(8,128)S(1)} %get-tuple-element.62), channel_id=1, source_target_pairs={{0,1},{1,0},{2,3},{3,2},{4,5},{5,4},{6,7},{7,6},{8,9},{9,8},{10,11... | collective-permute-start | bytes 221192 | tf_op jit(solution)/shard_map/ppermute | solution.py:588
  42.1 12.7 %collective-permute-start.5 = (f32[3,48,128]{2,1,0:T(8,128)S(1)}, f32[3,48,128]{2,1,0:T(8,128)S(1)}, u32[]{:S(2)}, u32[]{:S(2)}) collective-permute-start(f32[3,48,128]{2,1,0:T(8,128)S(1)} %get-tuple-element.58), channel_id=1, source_target_pairs={{0,32},{1,33},{2,34},{3,35},{4,36},{5,37},{6,38},{7,39},{8,40},{9,... | collective-permute-start | bytes 221192 | tf_op jit(solution)/shard_map/ppermute | solution.py:588
  43.7 11.1 %collective-permute-start.6 = (f32[3,48,128]{2,1,0:T(8,128)S(1)}, f32[3,48,128]{2,1,0:T(8,128)S(1)}, u32[]{:S(2)}, u32[]{:S(2)}) collective-permute-start(f32[3,48,128]{2,1,0:T(8,128)S(1)} %get-tuple-element.59), channel_id=1, source_target_pairs={{0,32},{1,2},{2,1},{3,4},{4,3},{5,6},{6,5},{7,8},{8,7},{9,10},{10,... | collective-permute-start | bytes 221192 | tf_op jit(solution)/shard_map/ppermute | solution.py:588
  43.7 11.1 %collective-permute-start.7 = (f32[3,48,128]{2,1,0:T(8,128)S(1)}, f32[3,48,128]{2,1,0:T(8,128)S(1)}, u32[]{:S(2)}, u32[]{:S(2)}) collective-permute-start(f32[3,48,128]{2,1,0:T(8,128)S(1)} %get-tuple-element.60), channel_id=1, source_target_pairs={{0,1},{1,0},{2,3},{3,2},{4,5},{5,4},{6,7},{7,6},{8,9},{9,8},{10,11... | collective-permute-start | bytes 221192 | tf_op jit(solution)/shard_map/ppermute | solution.py:588
  61.2 1.4 %collective-permute-start.12 = (f32[3,48,128]{2,1,0:T(8,128)S(1)}, f32[3,48,128]{2,1,0:T(8,128)S(1)}, u32[]{:S(2)}, u32[]{:S(2)}) collective-permute-start(f32[3,48,128]{2,1,0:T(8,128)S(1)} %get-tuple-element.70), channel_id=1, source_target_pairs={{0,1},{1,0},{2,3},{3,2},{4,5},{5,4},{6,7},{7,6},{8,9},{9,8},{10,11... | collective-permute-start | bytes 221192 | tf_op jit(solution)/shard_map/ppermute | solution.py:588
  61.3 7.3 %collective-permute-start.9 = (f32[3,48,128]{2,1,0:T(8,128)S(1)}, f32[3,48,128]{2,1,0:T(8,128)S(1)}, u32[]{:S(2)}, u32[]{:S(2)}) collective-permute-start(f32[3,48,128]{2,1,0:T(8,128)S(1)} %get-tuple-element.67), channel_id=1, source_target_pairs={{0,32},{1,33},{2,34},{3,35},{4,36},{5,37},{6,38},{7,39},{8,40},{9,... | collective-permute-start | bytes 221192 | tf_op jit(solution)/shard_map/ppermute | solution.py:588
  61.4 7.2 %collective-permute-start.10 = (f32[3,48,128]{2,1,0:T(8,128)S(1)}, f32[3,48,128]{2,1,0:T(8,128)S(1)}, u32[]{:S(2)}, u32[]{:S(2)}) collective-permute-start(f32[3,48,128]{2,1,0:T(8,128)S(1)} %get-tuple-element.68), channel_id=1, source_target_pairs={{0,32},{1,2},{2,1},{3,4},{4,3},{5,6},{6,5},{7,8},{8,7},{9,10},{10,... | collective-permute-start | bytes 221192 | tf_op jit(solution)/shard_map/ppermute | solution.py:588
  61.5 7.4 %collective-permute-start.11 = (f32[3,48,128]{2,1,0:T(8,128)S(1)}, f32[3,48,128]{2,1,0:T(8,128)S(1)}, u32[]{:S(2)}, u32[]{:S(2)}) collective-permute-start(f32[3,48,128]{2,1,0:T(8,128)S(1)} %get-tuple-element.69), channel_id=1, source_target_pairs={{0,1},{1,0},{2,3},{3,2},{4,5},{5,4},{6,7},{7,6},{8,9},{9,8},{10,11... | collective-permute-start | bytes 221192 | tf_op jit(solution)/shard_map/ppermute | solution.py:588
  75.3 3.6 %collective-permute-start.16 = (f32[3,48,128]{2,1,0:T(8,128)S(1)}, f32[3,48,128]{2,1,0:T(8,128)S(1)}, u32[]{:S(2)}, u32[]{:S(2)}) collective-permute-start(f32[3,48,128]{2,1,0:T(8,128)S(1)} %get-tuple-element.78), channel_id=1, source_target_pairs={{0,1},{1,0},{2,3},{3,2},{4,5},{5,4},{6,7},{7,6},{8,9},{9,8},{10,11... | collective-permute-start | bytes 221192 | tf_op jit(solution)/shard_map/ppermute | solution.py:588
  75.4 9.5 %collective-permute-start.13 = (f32[3,48,128]{2,1,0:T(8,128)S(1)}, f32[3,48,128]{2,1,0:T(8,128)S(1)}, u32[]{:S(2)}, u32[]{:S(2)}) collective-permute-start(f32[3,48,128]{2,1,0:T(8,128)S(1)} %get-tuple-element.75), channel_id=1, source_target_pairs={{0,32},{1,33},{2,34},{3,35},{4,36},{5,37},{6,38},{7,39},{8,40},{9,... | collective-permute-start | bytes 221192 | tf_op jit(solution)/shard_map/ppermute | solution.py:588
  75.5 9.4 %collective-permute-start.14 = (f32[3,48,128]{2,1,0:T(8,128)S(1)}, f32[3,48,128]{2,1,0:T(8,128)S(1)}, u32[]{:S(2)}, u32[]{:S(2)}) collective-permute-start(f32[3,48,128]{2,1,0:T(8,128)S(1)} %get-tuple-element.76), channel_id=1, source_target_pairs={{0,32},{1,2},{2,1},{3,4},{4,3},{5,6},{6,5},{7,8},{8,7},{9,10},{10,... | collective-permute-start | bytes 221192 | tf_op jit(solution)/shard_map/ppermute | solution.py:588
  77.5 8.1 %collective-permute-start.15 = (f32[3,48,128]{2,1,0:T(8,128)S(1)}, f32[3,48,128]{2,1,0:T(8,128)S(1)}, u32[]{:S(2)}, u32[]{:S(2)}) collective-permute-start(f32[3,48,128]{2,1,0:T(8,128)S(1)} %get-tuple-element.77), channel_id=1, source_target_pairs={{0,1},{1,0},{2,3},{3,2},{4,5},{5,4},{6,7},{7,6},{8,9},{9,8},{10,11... | collective-permute-start | bytes 221192 | tf_op jit(solution)/shard_map/ppermute | solution.py:588
  92.8 4.2 %collective-permute-start.20 = (f32[3,48,128]{2,1,0:T(8,128)S(1)}, f32[3,48,128]{2,1,0:T(8,128)S(1)}, u32[]{:S(2)}, u32[]{:S(2)}) collective-permute-start(f32[3,48,128]{2,1,0:T(8,128)S(1)} %get-tuple-element.87), channel_id=1, source_target_pairs={{0,1},{1,0},{2,3},{3,2},{4,5},{5,4},{6,7},{7,6},{8,9},{9,8},{10,11... | collective-permute-start | bytes 221192 | tf_op jit(solution)/shard_map/ppermute | solution.py:588
  93.1 9.7 %collective-permute-start.17 = (f32[3,48,128]{2,1,0:T(8,128)S(1)}, f32[3,48,128]{2,1,0:T(8,128)S(1)}, u32[]{:S(2)}, u32[]{:S(2)}) collective-permute-start(f32[3,48,128]{2,1,0:T(8,128)S(1)} %get-tuple-element.84), channel_id=1, source_target_pairs={{0,32},{1,33},{2,34},{3,35},{4,36},{5,37},{6,38},{7,39},{8,40},{9,... | collective-permute-start | bytes 221192 | tf_op jit(solution)/shard_map/ppermute | solution.py:588
  93.2 9.6 %collective-permute-start.18 = (f32[3,48,128]{2,1,0:T(8,128)S(1)}, f32[3,48,128]{2,1,0:T(8,128)S(1)}, u32[]{:S(2)}, u32[]{:S(2)}) collective-permute-start(f32[3,48,128]{2,1,0:T(8,128)S(1)} %get-tuple-element.85), channel_id=1, source_target_pairs={{0,32},{1,2},{2,1},{3,4},{4,3},{5,6},{6,5},{7,8},{8,7},{9,10},{10,... | collective-permute-start | bytes 221192 | tf_op jit(solution)/shard_map/ppermute | solution.py:588
  93.3 9.5 %collective-permute-start.19 = (f32[3,48,128]{2,1,0:T(8,128)S(1)}, f32[3,48,128]{2,1,0:T(8,128)S(1)}, u32[]{:S(2)}, u32[]{:S(2)}) collective-permute-start(f32[3,48,128]{2,1,0:T(8,128)S(1)} %get-tuple-element.86), channel_id=1, source_target_pairs={{0,1},{1,0},{2,3},{3,2},{4,5},{5,4},{6,7},{7,6},{8,9},{9,8},{10,11... | collective-permute-start | bytes 221192 | tf_op jit(solution)/shard_map/ppermute | solution.py:588

commit v3 on v1

--- a/solution.py
+++ b/solution.py
@@ -20,7 +20,7 @@
 AT_PAIRS = AT_SENDS + 4 * GHOST + LEAD
 LIST = BLOCKS * NEAR + TAIL + LEAD
 CONTROL = AT_PAIRS + 2 * LIST + 8
-EARLY, LATE = (3,), (0, 2, 1)
+EARLY, LATE = (3,), (1, 0, 2)
 SHARE = 9
 
 core_sq = 0.04
@@ -157,7 +157,7 @@
 
 
 def pack_kernel(
-    numbers, positions, burgers, places, scalars, s3, s0, s2, s1, numbers_smem, sem
+    numbers, positions, burgers, places, scalars, s3, s1, s0, s2, numbers_smem, sem
 ):
     copy = pltpu.make_async_copy(numbers, numbers_smem, sem)
     copy.start()
@@ -420,10 +420,20 @@
         half(2 * step + 1, k_odd, k_even)
         return carry
 
-    steps = (control[which] + 2 * GROUP - 1) // (2 * GROUP)
+    groups = lax.shift_right_logical(control[which] + GROUP - 1, 3)
+    steps = lax.shift_right_logical(groups, 1)
     lax.fori_loop(0, steps, body, 0)
-    for g in range(0, GROUP, 2):
-        sums(2 * steps - 1, g, k_odd)
+
+    @pl.when(groups == 2 * steps)
+    def _():
+        for g in range(0, GROUP, 2):
+            sums(2 * steps - 1, g, k_odd)
+
+    @pl.when(groups != 2 * steps)
+    def _():
+        half(2 * steps, k_even, k_odd)
+        for g in range(0, GROUP, 2):
+            sums(2 * steps, g, k_even)
 
 
 def component(acc, a):
@@ -453,7 +463,7 @@
 
 
 def first_kernel(
-    control_in, own, burgers, g3, g0, g2, g1, near, burg, control, sem, left, mask, k_even, k_odd, parts, right, acc
+    control_in, own, burgers, g3, g1, g0, g2, near, burg, control, sem, left, mask, k_even, k_odd, parts, right, acc
 ):
     copy = pltpu.make_async_copy(control_in, control, sem)
     copy.start()
@@ -512,7 +522,7 @@
 
 
 def late_force(
-    control_in, expansion, own, g0, g2, g1, burg, right, acc_in, control, sem, left, mask, k_even, k_odd, acc
+    control_in, expansion, own, g1, g0, g2, burg, right, acc_in, control, sem, left, mask, k_even, k_odd, acc
 ):
     copy = pltpu.make_async_copy(control_in, control, sem)
     copy.start()
@@ -526,10 +536,10 @@
 
 
 def step_kernel(
-    final, control, expansion, own, g0, g2, g1, burg, right, acc_in, mobility, places, moved,
+    final, control, expansion, own, g1, g0, g2, burg, right, acc_in, mobility, places, moved,
     new_moved, now, s0, s1, s2, s3, *scratch
 ):
-    force = late_force(control, expansion, own, g0, g2, g1, burg, right, acc_in, *scratch)
+    force = late_force(control, expansion, own, g1, g0, g2, burg, right, acc_in, *scratch)
     for a in range(3):
         total = moved[a] + (time_step * mobility[...]) * force[a]
         if final:
@@ -541,9 +551,9 @@
 
 
 def last_kernel(
-    control, expansion, own, g0, g2, g1, burg, right, acc_in, mobility, velocity, *scratch
+    control, expansion, own, g1, g0, g2, burg, right, acc_in, mobility, velocity, *scratch
 ):
-    force = late_force(control, expansion, own, g0, g2, g1, burg, right, acc_in, *scratch)
+    force = late_force(control, expansion, own, g1, g0, g2, burg, right, acc_in, *scratch)
     for a in range(3):
         put_rows(velocity, a, mobility[...] * force[a])
 
@@ -602,7 +612,7 @@
         compiler_params=params,
         name="pack",
     )(numbers, positions, burgers)
-    ghosts = [swap(x, slot) for x, slot in zip(sends, (3, 0, 2, 1))]
+    ghosts = [swap(x, slot) for x, slot in zip(sends, EARLY + LATE)]
 
     shares, control = pl.pallas_call(
         far_kernel,

time: 107 us -> 107 us (level)
  the two profiles are of different devices: /device:TPU:9 before, /device:TPU:15 now
where the time goes in v3:
time: 107 us
  Pallas kernels  67.2 us (63%)
  starting transfers between devices  36.8 us (34%)
  between operations  1.14 us (1%)
    pallas_call x4, Pallas kernels, evaluate(): pl.pallas_call(kernel, out_shape=out_shape, in_specs=[vmem] * (7 + len(LA...  24.4 us
    ppermute x20, starting transfers between devices, swap(): return lax.ppermute(x, ('slab', 'cell'), pairs)  24.3 us
    pallas_call x4, Pallas kernels, evaluate(): pl.pallas_call(early_kernel, out_shape=[shape(*right_shape, dtype=bf16),...  22.8 us
    all_to_all x1, starting transfers between devices, local(): shares = lax.all_to_all(shares, ('slab', 'cell'), 0, 0, tiled=True)  12.6 us
    pallas_call x1, Pallas kernels, local(): pl.pallas_call(first_kernel, out_shape=[block, shape((EXT + 1) * 8, LANES...  10.6 us
    pallas_call x1, Pallas kernels, local(): pl.pallas_call(far_kernel, out_shape=[shape(EXT, LANES), shape(CONTROL, d...  7.12 us
  transfers between devices with their start and end apart: 21, of which 0 were waited for; matrix products, arithmetic and copies ran while one was open for 0% of the time, Pallas kernels for 38%

profile of v3, /device:TPU:15, one launch (start us, length us, event | category | flops | bytes accessed | tf_op | source)
XLA Modules:
  0.0 107.0 jit_solution(11215879969469194715)
XLA Ops:
  0.6 1.0 copy_bitcast_fusion
  1.6 0.7 pad_add_fusion.numbers
  2.3 1.4 %pack.1 = (f32[3,64,128]{2,1,0:T(8,128)S(1)}, s32[16,128]{1,0:T(8,128)S(1)}, f32[6,48,128]{2,1,0:T(8,128)S(1)}, f32[6,48,128]{2,1,0:T(8,128)S(1)}, f32[6,48,128]{2,1,0:T(8,128)S(1)}, /*index=5*/f32[6,48,128]{2,1,0:T(8,128)S(1)}) custom-call(s32[16,128]{1,0:T(8,128)S(1)} %pad_add_fusion.numbers, f32[3,64,128]{2,1,0:T(8,128)S(1)} %get-tuple-element.89.positions, ...), custom_call_target="tpu_custom_call" | custom-call | tf_op jit(solution)/shard_map/pack/pallas_call | solution.py:606
  3.7 0.8 collective-permute-start
  4.5 1.3 %collective-permute-start.1 = (f32[6,48,128]{2,1,0:T(8,128)S(1)}, f32[6,48,128]{2,1,0:T(8,128)S(1)}, u32[]{:S(2)}, u32[]{:S(2)}) collective-permute-start(f32[6,48,128]{2,1,0:T(8,128)S(1)} %get-tuple-element.50), channel_id=1, source_target_pairs={{0,1},{1,0},{2,3},{3,2},{4,5},{5,4},{6,7},{7,6},{8,9},{9,8},{10,11... | collective-permute-start | bytes 442376 | tf_op jit(solution)/shard_map/ppermute | solution.py:585
  5.8 2.4 %collective-permute-start.2 = (f32[6,48,128]{2,1,0:T(8,128)S(1)}, f32[6,48,128]{2,1,0:T(8,128)S(1)}, u32[]{:S(2)}, u32[]{:S(2)}) collective-permute-start(f32[6,48,128]{2,1,0:T(8,128)S(1)} %get-tuple-element.51), channel_id=1, source_target_pairs={{0,32},{1,33},{2,34},{3,35},{4,36},{5,37},{6,38},{7,39},{8,40},{9,... | collective-permute-start | bytes 442376 | tf_op jit(solution)/shard_map/ppermute | solution.py:585
  8.3 1.5 %collective-permute-start.3 = (f32[6,48,128]{2,1,0:T(8,128)S(1)}, f32[6,48,128]{2,1,0:T(8,128)S(1)}, u32[]{:S(2)}, u32[]{:S(2)}) collective-permute-start(f32[6,48,128]{2,1,0:T(8,128)S(1)} %get-tuple-element.52), channel_id=1, source_target_pairs={{0,32},{1,2},{2,1},{3,4},{4,3},{5,6},{6,5},{7,8},{8,7},{9,10},{10,... | collective-permute-start | bytes 442376 | tf_op jit(solution)/shard_map/ppermute | solution.py:585
  9.8 7.1 %far.1 = (f32[256,128]{1,0:T(8,128)}, s32[1112]{0:T(1024)S(1)}) custom-call(s32[16,128]{1,0:T(8,128)S(1)} %get-tuple-element.45.scalars_in, f32[3,64,128]{2,1,0:T(8,128)S(1)} %get-tuple-element.46.places.own, f32[3,64,128]{2,1,0:T(8,128)S(1)} %get-tuple-element.88.burgers), custom_call_target="tpu_custom_call" | custom-call | flops 20000000000 | bytes 1048576 | tf_op jit(solution)/shard_map/far/pallas_call | solution.py:617
  16.9 12.6 %all-to-all-start = ((f32[256,1,128]{2,1,0:T(1,128)}), f32[256,1,128]{2,1,0:T(1,128)S(1)}, u32[]{:S(2)}, u32[]{:S(2)}) async-start(f32[256,1,128]{2,1,0:T(1,128)} %bitcast.3), calls=%async_computation | async-start | bytes 262144 | tf_op jit(solution)/shard_map/all_to_all | solution.py:637
  29.6 10.6 %near_first.1 = (f32[3,64,128]{2,1,0:T(8,128)S(1)}, f32[2056,128]{1,0:T(8,128)S(1)}) custom-call(s32[1112]{0:T(1024)S(1)} %get-tuple-element.47.control_in.control, f32[3,64,128]{2,1,0:T(8,128)S(1)} %get-tuple-element.46.places.own, f32[3,64,128]{2,1,0:T(8,128)S(1)} %get-tuple-element.88.burgers, f32[6,48,128]{2,1,0:T(8,128)S(1)} %collective-permute-done.g3, ...), custom_call_target="tpu_custom_call" | custom-call | flops 20000000000 | bytes 1048576 | tf_op jit(solution)/shard_map/near_first/pallas_call | solution.py:639
  40.2 1.0 start.1
  41.8 2.9 %collective-permute-start.5 = (f32[3,48,128]{2,1,0:T(8,128)S(1)}, f32[3,48,128]{2,1,0:T(8,128)S(1)}, u32[]{:S(2)}, u32[]{:S(2)}) collective-permute-start(f32[3,48,128]{2,1,0:T(8,128)S(1)} %get-tuple-element.57), channel_id=1, source_target_pairs={{0,32},{1,33},{2,34},{3,35},{4,36},{5,37},{6,38},{7,39},{8,40},{9,... | collective-permute-start | bytes 221192 | tf_op jit(solution)/shard_map/ppermute | solution.py:585
  44.7 2.0 %collective-permute-start.6 = (f32[3,48,128]{2,1,0:T(8,128)S(1)}, f32[3,48,128]{2,1,0:T(8,128)S(1)}, u32[]{:S(2)}, u32[]{:S(2)}) collective-permute-start(f32[3,48,128]{2,1,0:T(8,128)S(1)} %get-tuple-element.58), channel_id=1, source_target_pairs={{0,32},{1,2},{2,1},{3,4},{4,3},{5,6},{6,5},{7,8},{8,7},{9,10},{10,... | collective-permute-start | bytes 221192 | tf_op jit(solution)/shard_map/ppermute | solution.py:585
  46.7 5.8 %near_early.4 = (bf16[64,8,16,128]{3,2,1,0:T(8,128)(2,1)S(1)}, f32[512,128]{1,0:T(8,128)S(1)}) custom-call(s32[1112]{0:T(1024)S(1)} %get-tuple-element.47.control_in.control, f32[3,64,128]{2,1,0:T(8,128)S(1)} %get-tuple-element.55.own, f32[3,48,128]{2,1,0:T(8,128)S(1)} %collective-permute-done.7.g3, f32[2056,128]{1,0:T(8,128)S(1)} %get-tuple-element.59.burg), custom_call_target="tpu_custom_call" | custom-call | flops 20000000000 | bytes 1048576 | tf_op jit(solution)/shard_map/near_early/pallas_call | solution.py:663
  52.6 5.8 %near_step.3 = (f32[3,64,128]{2,1,0:T(8,128)S(1)}, f32[3,64,128]{2,1,0:T(8,128)S(1)}, f32[3,48,128]{2,1,0:T(8,128)S(1)}, f32[3,48,128]{2,1,0:T(8,128)S(1)}, f32[...) custom-call(s32[1112]{0:T(1024)S(1)} %get-tuple-element.47.control_in.control, ...), custom_call_target="tpu_custom_call" | custom-call | flops 10000000000 | bytes 1048576 | tf_op jit(solution)/shard_map/near_step/pallas_call | solution.py:673
  58.7 3.6 %collective-permute-start.10 = (f32[3,48,128]{2,1,0:T(8,128)S(1)}, f32[3,48,128]{2,1,0:T(8,128)S(1)}, u32[]{:S(2)}, u32[]{:S(2)}) collective-permute-start(f32[3,48,128]{2,1,0:T(8,128)S(1)} %get-tuple-element.67), channel_id=1, source_target_pairs={{0,32},{1,2},{2,1},{3,4},{4,3},{5,6},{6,5},{7,8},{8,7},{9,10},{10,... | collective-permute-start | bytes 221192 | tf_op jit(solution)/shard_map/ppermute | solution.py:585
  62.3 5.6 %near_early.5 = (bf16[64,8,16,128]{3,2,1,0:T(8,128)(2,1)S(1)}, f32[512,128]{1,0:T(8,128)S(1)}) custom-call(s32[1112]{0:T(1024)S(1)} %get-tuple-element.47.control_in.control, f32[3,64,128]{2,1,0:T(8,128)S(1)} %get-tuple-element.64.own, f32[3,48,128]{2,1,0:T(8,128)S(1)} %collective-permute-done.11.g3, f32[2056,128]{1,0:T(8,128)S(1)} %get-tuple-element.59.burg), custom_call_target="tpu_custom_call" | custom-call | flops 20000000000 | bytes 1048576 | tf_op jit(solution)/shard_map/near_early/pallas_call | solution.py:663
  68.0 5.8 %near_step.4 = (f32[3,64,128]{2,1,0:T(8,128)S(1)}, f32[3,64,128]{2,1,0:T(8,128)S(1)}, f32[3,48,128]{2,1,0:T(8,128)S(1)}, f32[3,48,128]{2,1,0:T(8,128)S(1)}, f32[...) custom-call(s32[1112]{0:T(1024)S(1)} %get-tuple-element.47.control_in.control, ...), custom_call_target="tpu_custom_call" | custom-call | flops 10000000000 | bytes 1048576 | tf_op jit(solution)/shard_map/near_step/pallas_call | solution.py:673
  74.1 4.0 %collective-permute-start.14 = (f32[3,48,128]{2,1,0:T(8,128)S(1)}, f32[3,48,128]{2,1,0:T(8,128)S(1)}, u32[]{:S(2)}, u32[]{:S(2)}) collective-permute-start(f32[3,48,128]{2,1,0:T(8,128)S(1)} %get-tuple-element.75), channel_id=1, source_target_pairs={{0,32},{1,2},{2,1},{3,4},{4,3},{5,6},{6,5},{7,8},{8,7},{9,10},{10,... | collective-permute-start | bytes 221192 | tf_op jit(solution)/shard_map/ppermute | solution.py:585
  78.2 5.8 %near_early.6 = (bf16[64,8,16,128]{3,2,1,0:T(8,128)(2,1)S(1)}, f32[512,128]{1,0:T(8,128)S(1)}) custom-call(s32[1112]{0:T(1024)S(1)} %get-tuple-element.47.control_in.control, f32[3,64,128]{2,1,0:T(8,128)S(1)} %get-tuple-element.72.own, f32[3,48,128]{2,1,0:T(8,128)S(1)} %collective-permute-done.15.g3, f32[2056,128]{1,0:T(8,128)S(1)} %get-tuple-element.59.burg), custom_call_target="tpu_custom_call" | custom-call | flops 20000000000 | bytes 1048576 | tf_op jit(solution)/shard_map/near_early/pallas_call | solution.py:663
  84.0 6.5 %near_step.5 = (f32[3,8192]{1,0:T(4,128)}, f32[3,64,128]{2,1,0:T(8,128)S(1)}, f32[3,48,128]{2,1,0:T(8,128)S(1)}, f32[3,48,128]{2,1,0:T(8,128)S(1)}, f32[3,48,128...) custom-call(s32[1112]{0:T(1024)S(1)} %get-tuple-element.47.control_in.control, f32[8,128]{1,0:T(8,128)S(1)} %get-tuple-element.54.expansion, ...), custom_call_target="tpu_custom_call" | custom-call | flops 10000000000 | bytes 1048576 | tf_op jit(solution)/shard_map/near_step/pallas_call | solution.py:673
  90.8 4.2 %collective-permute-start.18 = (f32[3,48,128]{2,1,0:T(8,128)S(1)}, f32[3,48,128]{2,1,0:T(8,128)S(1)}, u32[]{:S(2)}, u32[]{:S(2)}) collective-permute-start(f32[3,48,128]{2,1,0:T(8,128)S(1)} %get-tuple-element.84), channel_id=1, source_target_pairs={{0,32},{1,2},{2,1},{3,4},{4,3},{5,6},{6,5},{7,8},{8,7},{9,10},{10,... | collective-permute-start | bytes 221192 | tf_op jit(solution)/shard_map/ppermute | solution.py:585
  95.0 5.5 %near_early.7 = (bf16[64,8,16,128]{3,2,1,0:T(8,128)(2,1)S(1)}, f32[512,128]{1,0:T(8,128)S(1)}) custom-call(s32[1112]{0:T(1024)S(1)} %get-tuple-element.47.control_in.control, f32[3,64,128]{2,1,0:T(8,128)S(1)} %get-tuple-element.81.own, f32[3,48,128]{2,1,0:T(8,128)S(1)} %collective-permute-done.19.g3, f32[2056,128]{1,0:T(8,128)S(1)} %get-tuple-element.59.burg), custom_call_target="tpu_custom_call" | custom-call | flops 20000000000 | bytes 1048576 | tf_op jit(solution)/shard_map/near_early/pallas_call | solution.py:663
  100.6 6.2 %near_last.1 = f32[3,8192]{1,0:T(4,128)} custom-call(s32[1112]{0:T(1024)S(1)} %get-tuple-element.47.control_in.control, f32[8,128]{1,0:T(8,128)S(1)} %get-tuple-element.54.expansion, f32[3,64,128]{2,1,0:T(8,128)S(1)} %get-tuple-element.81.own, f32[3,48,128]{2,1,0:T(8,128)S(1)} %collective-permute-done.16.g1, f32[3,48,128]{2,1,0:T(8,128)S(1)} %collective-permute-done.17.g0, ...), custom_call_target="tpu_custom_call" | custom-call | flops 10000000000 | bytes 1048576 | tf_op jit(solution)/shard_map/near_last/pallas_call | solution.py:673
  (34 shorter events, 1.5 us)
Async XLA Ops:
  3.7 25.8 %collective-permute-start = (f32[6,48,128]{2,1,0:T(8,128)S(1)}, f32[6,48,128]{2,1,0:T(8,128)S(1)}, u32[]{:S(2)}, u32[]{:S(2)}) collective-permute-start(f32[6,48,128]{2,1,0:T(8,128)S(1)} %get-tuple-element.49), channel_id=1, source_target_pairs={{0,1},{1,0},{2,3},{3,2},{4,5},{5,4},{6,7},{7,6},{8,9},{9,8},{10,11... | collective-permute-start | bytes 442376 | tf_op jit(solution)/shard_map/ppermute | solution.py:585
  4.5 25.0 %collective-permute-start.1 = (f32[6,48,128]{2,1,0:T(8,128)S(1)}, f32[6,48,128]{2,1,0:T(8,128)S(1)}, u32[]{:S(2)}, u32[]{:S(2)}) collective-permute-start(f32[6,48,128]{2,1,0:T(8,128)S(1)} %get-tuple-element.50), channel_id=1, source_target_pairs={{0,1},{1,0},{2,3},{3,2},{4,5},{5,4},{6,7},{7,6},{8,9},{9,8},{10,11... | collective-permute-start | bytes 442376 | tf_op jit(solution)/shard_map/ppermute | solution.py:585
  5.8 23.7 %collective-permute-start.2 = (f32[6,48,128]{2,1,0:T(8,128)S(1)}, f32[6,48,128]{2,1,0:T(8,128)S(1)}, u32[]{:S(2)}, u32[]{:S(2)}) collective-permute-start(f32[6,48,128]{2,1,0:T(8,128)S(1)} %get-tuple-element.51), channel_id=1, source_target_pairs={{0,32},{1,33},{2,34},{3,35},{4,36},{5,37},{6,38},{7,39},{8,40},{9,... | collective-permute-start | bytes 442376 | tf_op jit(solution)/shard_map/ppermute | solution.py:585
  8.3 21.3 %collective-permute-start.3 = (f32[6,48,128]{2,1,0:T(8,128)S(1)}, f32[6,48,128]{2,1,0:T(8,128)S(1)}, u32[]{:S(2)}, u32[]{:S(2)}) collective-permute-start(f32[6,48,128]{2,1,0:T(8,128)S(1)} %get-tuple-element.52), channel_id=1, source_target_pairs={{0,32},{1,2},{2,1},{3,4},{4,3},{5,6},{6,5},{7,8},{8,7},{9,10},{10,... | collective-permute-start | bytes 442376 | tf_op jit(solution)/shard_map/ppermute | solution.py:585
  16.9 23.3 %all-to-all-start = ((f32[256,1,128]{2,1,0:T(1,128)}), f32[256,1,128]{2,1,0:T(1,128)S(1)}, u32[]{:S(2)}, u32[]{:S(2)}) async-start(f32[256,1,128]{2,1,0:T(1,128)} %bitcast.3), calls=%async_computation | async-start | bytes 262144 | tf_op jit(solution)/shard_map/all_to_all | solution.py:637
  29.6 10.6 %copy-start = (f32[8192]{0:T(1024)S(1)}, f32[8192]{0:T(1024)}, u32[]{:S(2)}) copy-start(f32[8192]{0:T(1024)} %param.8) | copy-start | bytes 98308
  41.2 5.5 %collective-permute-start.7 = (f32[3,48,128]{2,1,0:T(8,128)S(1)}, f32[3,48,128]{2,1,0:T(8,128)S(1)}, u32[]{:S(2)}, u32[]{:S(2)}) collective-permute-start(f32[3,48,128]{2,1,0:T(8,128)S(1)} %get-tuple-element.60), channel_id=1, source_target_pairs={{0,1},{1,0},{2,3},{3,2},{4,5},{5,4},{6,7},{7,6},{8,9},{9,8},{10,11... | collective-permute-start | bytes 221192 | tf_op jit(solution)/shard_map/ppermute | solution.py:585
  41.7 10.8 %collective-permute-start.4 = (f32[3,48,128]{2,1,0:T(8,128)S(1)}, f32[3,48,128]{2,1,0:T(8,128)S(1)}, u32[]{:S(2)}, u32[]{:S(2)}) collective-permute-start(f32[3,48,128]{2,1,0:T(8,128)S(1)} %get-tuple-element.56), channel_id=1, source_target_pairs={{0,1},{1,0},{2,3},{3,2},{4,5},{5,4},{6,7},{7,6},{8,9},{9,8},{10,11... | collective-permute-start | bytes 221192 | tf_op jit(solution)/shard_map/ppermute | solution.py:585
  41.8 10.7 %collective-permute-start.5 = (f32[3,48,128]{2,1,0:T(8,128)S(1)}, f32[3,48,128]{2,1,0:T(8,128)S(1)}, u32[]{:S(2)}, u32[]{:S(2)}) collective-permute-start(f32[3,48,128]{2,1,0:T(8,128)S(1)} %get-tuple-element.57), channel_id=1, source_target_pairs={{0,32},{1,33},{2,34},{3,35},{4,36},{5,37},{6,38},{7,39},{8,40},{9,... | collective-permute-start | bytes 221192 | tf_op jit(solution)/shard_map/ppermute | solution.py:585
  44.7 7.9 %collective-permute-start.6 = (f32[3,48,128]{2,1,0:T(8,128)S(1)}, f32[3,48,128]{2,1,0:T(8,128)S(1)}, u32[]{:S(2)}, u32[]{:S(2)}) collective-permute-start(f32[3,48,128]{2,1,0:T(8,128)S(1)} %get-tuple-element.58), channel_id=1, source_target_pairs={{0,32},{1,2},{2,1},{3,4},{4,3},{5,6},{6,5},{7,8},{8,7},{9,10},{10,... | collective-permute-start | bytes 221192 | tf_op jit(solution)/shard_map/ppermute | solution.py:585
  58.4 3.9 %collective-permute-start.11 = (f32[3,48,128]{2,1,0:T(8,128)S(1)}, f32[3,48,128]{2,1,0:T(8,128)S(1)}, u32[]{:S(2)}, u32[]{:S(2)}) collective-permute-start(f32[3,48,128]{2,1,0:T(8,128)S(1)} %get-tuple-element.68), channel_id=1, source_target_pairs={{0,1},{1,0},{2,3},{3,2},{4,5},{5,4},{6,7},{7,6},{8,9},{9,8},{10,11... | collective-permute-start | bytes 221192 | tf_op jit(solution)/shard_map/ppermute | solution.py:585
  58.5 9.5 %collective-permute-start.8 = (f32[3,48,128]{2,1,0:T(8,128)S(1)}, f32[3,48,128]{2,1,0:T(8,128)S(1)}, u32[]{:S(2)}, u32[]{:S(2)}) collective-permute-start(f32[3,48,128]{2,1,0:T(8,128)S(1)} %get-tuple-element.65), channel_id=1, source_target_pairs={{0,1},{1,0},{2,3},{3,2},{4,5},{5,4},{6,7},{7,6},{8,9},{9,8},{10,11... | collective-permute-start | bytes 221192 | tf_op jit(solution)/shard_map/ppermute | solution.py:585
  58.6 9.4 %collective-permute-start.9 = (f32[3,48,128]{2,1,0:T(8,128)S(1)}, f32[3,48,128]{2,1,0:T(8,128)S(1)}, u32[]{:S(2)}, u32[]{:S(2)}) collective-permute-start(f32[3,48,128]{2,1,0:T(8,128)S(1)} %get-tuple-element.66), channel_id=1, source_target_pairs={{0,32},{1,33},{2,34},{3,35},{4,36},{5,37},{6,38},{7,39},{8,40},{9,... | collective-permute-start | bytes 221192 | tf_op jit(solution)/shard_map/ppermute | solution.py:585
  58.7 9.3 %collective-permute-start.10 = (f32[3,48,128]{2,1,0:T(8,128)S(1)}, f32[3,48,128]{2,1,0:T(8,128)S(1)}, u32[]{:S(2)}, u32[]{:S(2)}) collective-permute-start(f32[3,48,128]{2,1,0:T(8,128)S(1)} %get-tuple-element.67), channel_id=1, source_target_pairs={{0,32},{1,2},{2,1},{3,4},{4,3},{5,6},{6,5},{7,8},{8,7},{9,10},{10,... | collective-permute-start | bytes 221192 | tf_op jit(solution)/shard_map/ppermute | solution.py:585
  73.8 4.3 %collective-permute-start.15 = (f32[3,48,128]{2,1,0:T(8,128)S(1)}, f32[3,48,128]{2,1,0:T(8,128)S(1)}, u32[]{:S(2)}, u32[]{:S(2)}) collective-permute-start(f32[3,48,128]{2,1,0:T(8,128)S(1)} %get-tuple-element.76), channel_id=1, source_target_pairs={{0,1},{1,0},{2,3},{3,2},{4,5},{5,4},{6,7},{7,6},{8,9},{9,8},{10,11... | collective-permute-start | bytes 221192 | tf_op jit(solution)/shard_map/ppermute | solution.py:585
  73.9 10.0 %collective-permute-start.12 = (f32[3,48,128]{2,1,0:T(8,128)S(1)}, f32[3,48,128]{2,1,0:T(8,128)S(1)}, u32[]{:S(2)}, u32[]{:S(2)}) collective-permute-start(f32[3,48,128]{2,1,0:T(8,128)S(1)} %get-tuple-element.73), channel_id=1, source_target_pairs={{0,1},{1,0},{2,3},{3,2},{4,5},{5,4},{6,7},{7,6},{8,9},{9,8},{10,11... | collective-permute-start | bytes 221192 | tf_op jit(solution)/shard_map/ppermute | solution.py:585
  74.0 9.9 %collective-permute-start.13 = (f32[3,48,128]{2,1,0:T(8,128)S(1)}, f32[3,48,128]{2,1,0:T(8,128)S(1)}, u32[]{:S(2)}, u32[]{:S(2)}) collective-permute-start(f32[3,48,128]{2,1,0:T(8,128)S(1)} %get-tuple-element.74), channel_id=1, source_target_pairs={{0,32},{1,33},{2,34},{3,35},{4,36},{5,37},{6,38},{7,39},{8,40},{9,... | collective-permute-start | bytes 221192 | tf_op jit(solution)/shard_map/ppermute | solution.py:585
  74.1 9.8 %collective-permute-start.14 = (f32[3,48,128]{2,1,0:T(8,128)S(1)}, f32[3,48,128]{2,1,0:T(8,128)S(1)}, u32[]{:S(2)}, u32[]{:S(2)}) collective-permute-start(f32[3,48,128]{2,1,0:T(8,128)S(1)} %get-tuple-element.75), channel_id=1, source_target_pairs={{0,32},{1,2},{2,1},{3,4},{4,3},{5,6},{6,5},{7,8},{8,7},{9,10},{10,... | collective-permute-start | bytes 221192 | tf_op jit(solution)/shard_map/ppermute | solution.py:585
  90.5 4.5 %collective-permute-start.19 = (f32[3,48,128]{2,1,0:T(8,128)S(1)}, f32[3,48,128]{2,1,0:T(8,128)S(1)}, u32[]{:S(2)}, u32[]{:S(2)}) collective-permute-start(f32[3,48,128]{2,1,0:T(8,128)S(1)} %get-tuple-element.85), channel_id=1, source_target_pairs={{0,1},{1,0},{2,3},{3,2},{4,5},{5,4},{6,7},{7,6},{8,9},{9,8},{10,11... | collective-permute-start | bytes 221192 | tf_op jit(solution)/shard_map/ppermute | solution.py:585
  90.6 9.9 %collective-permute-start.16 = (f32[3,48,128]{2,1,0:T(8,128)S(1)}, f32[3,48,128]{2,1,0:T(8,128)S(1)}, u32[]{:S(2)}, u32[]{:S(2)}) collective-permute-start(f32[3,48,128]{2,1,0:T(8,128)S(1)} %get-tuple-element.82), channel_id=1, source_target_pairs={{0,1},{1,0},{2,3},{3,2},{4,5},{5,4},{6,7},{7,6},{8,9},{9,8},{10,11... | collective-permute-start | bytes 221192 | tf_op jit(solution)/shard_map/ppermute | solution.py:585
  90.7 9.9 %collective-permute-start.17 = (f32[3,48,128]{2,1,0:T(8,128)S(1)}, f32[3,48,128]{2,1,0:T(8,128)S(1)}, u32[]{:S(2)}, u32[]{:S(2)}) collective-permute-start(f32[3,48,128]{2,1,0:T(8,128)S(1)} %get-tuple-element.83), channel_id=1, source_target_pairs={{0,32},{1,33},{2,34},{3,35},{4,36},{5,37},{6,38},{7,39},{8,40},{9,... | collective-permute-start | bytes 221192 | tf_op jit(solution)/shard_map/ppermute | solution.py:585
  90.8 9.8 %collective-permute-start.18 = (f32[3,48,128]{2,1,0:T(8,128)S(1)}, f32[3,48,128]{2,1,0:T(8,128)S(1)}, u32[]{:S(2)}, u32[]{:S(2)}) collective-permute-start(f32[3,48,128]{2,1,0:T(8,128)S(1)} %get-tuple-element.84), channel_id=1, source_target_pairs={{0,32},{1,2},{2,1},{3,4},{4,3},{5,6},{6,5},{7,8},{8,7},{9,10},{10,... | collective-permute-start | bytes 221192 | tf_op jit(solution)/shard_map/ppermute | solution.py:585

commit v4 on v1

--- a/solution.py
+++ b/solution.py
@@ -420,10 +420,20 @@
         half(2 * step + 1, k_odd, k_even)
         return carry
 
-    steps = (control[which] + 2 * GROUP - 1) // (2 * GROUP)
+    groups = lax.shift_right_logical(control[which] + GROUP - 1, 3)
+    steps = lax.shift_right_logical(groups, 1)
     lax.fori_loop(0, steps, body, 0)
-    for g in range(0, GROUP, 2):
-        sums(2 * steps - 1, g, k_odd)
+
+    @pl.when(groups == 2 * steps)
+    def _():
+        for g in range(0, GROUP, 2):
+            sums(2 * steps - 1, g, k_odd)
+
+    @pl.when(groups != 2 * steps)
+    def _():
+        half(2 * steps, k_even, k_odd)
+        for g in range(0, GROUP, 2):
+            sums(2 * steps, g, k_even)
 
 
 def component(acc, a):

time: 107 us -> 109 us (1.019)
  the two profiles are of different devices: /device:TPU:9 before, /device:TPU:71 now
where the time goes in v4:
time: 109 us; the launch traced here: 110 us
  Pallas kernels  69 us (63%)
  starting transfers between devices  37.7 us (35%)
  between operations  1.16 us (1%)
    pallas_call x4, Pallas kernels, evaluate(): pl.pallas_call(kernel, out_shape=out_shape, in_specs=[vmem] * (7 + len(LA...  28.3 us
    ppermute x20, starting transfers between devices, swap(): return lax.ppermute(x, ('slab', 'cell'), pairs)  27.1 us
    pallas_call x4, Pallas kernels, evaluate(): pl.pallas_call(early_kernel, out_shape=[shape(*right_shape, dtype=bf16),...  20.2 us
    pallas_call x1, Pallas kernels, local(): pl.pallas_call(first_kernel, out_shape=[block, shape((EXT + 1) * 8, LANES...  11 us
    all_to_all x1, starting transfers between devices, local(): shares = lax.all_to_all(shares, ('slab', 'cell'), 0, 0, tiled=True)  10.6 us
    pallas_call x1, Pallas kernels, local(): pl.pallas_call(far_kernel, out_shape=[shape(EXT, LANES), shape(CONTROL, d...  7.12 us
  transfers between devices with their start and end apart: 21, of which 0 were waited for; matrix products, arithmetic and copies ran while one was open for 0% of the time, Pallas kernels for 35%

profile of v4, /device:TPU:71, one launch (start us, length us, event | category | flops | bytes accessed | tf_op | source)
XLA Modules:
  0.0 109.6 jit_solution(4226311410802225447)
XLA Ops:
  0.6 1.0 copy_bitcast_fusion
  1.6 0.7 pad_add_fusion.numbers
  2.3 1.4 %pack.1 = (f32[3,64,128]{2,1,0:T(8,128)S(1)}, s32[16,128]{1,0:T(8,128)S(1)}, f32[6,48,128]{2,1,0:T(8,128)S(1)}, f32[6,48,128]{2,1,0:T(8,128)S(1)}, f32[6,48,128]{2,1,0:T(8,128)S(1)}, /*index=5*/f32[6,48,128]{2,1,0:T(8,128)S(1)}) custom-call(s32[16,128]{1,0:T(8,128)S(1)} %pad_add_fusion.numbers, f32[3,64,128]{2,1,0:T(8,128)S(1)} %get-tuple-element.89.positions, ...), custom_call_target="tpu_custom_call" | custom-call | tf_op jit(solution)/shard_map/pack/pallas_call | solution.py:606
  3.7 0.8 collective-permute-start
  4.5 1.3 %collective-permute-start.1 = (f32[6,48,128]{2,1,0:T(8,128)S(1)}, f32[6,48,128]{2,1,0:T(8,128)S(1)}, u32[]{:S(2)}, u32[]{:S(2)}) collective-permute-start(f32[6,48,128]{2,1,0:T(8,128)S(1)} %get-tuple-element.50), channel_id=1, source_target_pairs={{0,32},{1,33},{2,34},{3,35},{4,36},{5,37},{6,38},{7,39},{8,40},{9,... | collective-permute-start | bytes 442376 | tf_op jit(solution)/shard_map/ppermute | solution.py:585
  5.8 2.1 %collective-permute-start.2 = (f32[6,48,128]{2,1,0:T(8,128)S(1)}, f32[6,48,128]{2,1,0:T(8,128)S(1)}, u32[]{:S(2)}, u32[]{:S(2)}) collective-permute-start(f32[6,48,128]{2,1,0:T(8,128)S(1)} %get-tuple-element.51), channel_id=1, source_target_pairs={{0,32},{1,2},{2,1},{3,4},{4,3},{5,6},{6,5},{7,8},{8,7},{9,10},{10,... | collective-permute-start | bytes 442376 | tf_op jit(solution)/shard_map/ppermute | solution.py:585
  8.0 2.4 %collective-permute-start.3 = (f32[6,48,128]{2,1,0:T(8,128)S(1)}, f32[6,48,128]{2,1,0:T(8,128)S(1)}, u32[]{:S(2)}, u32[]{:S(2)}) collective-permute-start(f32[6,48,128]{2,1,0:T(8,128)S(1)} %get-tuple-element.52), channel_id=1, source_target_pairs={{0,1},{1,0},{2,3},{3,2},{4,5},{5,4},{6,7},{7,6},{8,9},{9,8},{10,11... | collective-permute-start | bytes 442376 | tf_op jit(solution)/shard_map/ppermute | solution.py:585
  10.4 7.1 %far.1 = (f32[256,128]{1,0:T(8,128)}, s32[1112]{0:T(1024)S(1)}) custom-call(s32[16,128]{1,0:T(8,128)S(1)} %get-tuple-element.45.scalars_in, f32[3,64,128]{2,1,0:T(8,128)S(1)} %get-tuple-element.46.places.own, f32[3,64,128]{2,1,0:T(8,128)S(1)} %get-tuple-element.88.burgers), custom_call_target="tpu_custom_call" | custom-call | flops 20000000000 | bytes 1048576 | tf_op jit(solution)/shard_map/far/pallas_call | solution.py:617
  17.5 10.6 %all-to-all-start = ((f32[256,1,128]{2,1,0:T(1,128)}), f32[256,1,128]{2,1,0:T(1,128)S(1)}, u32[]{:S(2)}, u32[]{:S(2)}) async-start(f32[256,1,128]{2,1,0:T(1,128)} %bitcast.3), calls=%async_computation | async-start | bytes 262144 | tf_op jit(solution)/shard_map/all_to_all | solution.py:637
  28.2 11.0 %near_first.1 = (f32[3,64,128]{2,1,0:T(8,128)S(1)}, f32[2056,128]{1,0:T(8,128)S(1)}) custom-call(s32[1112]{0:T(1024)S(1)} %get-tuple-element.47.control_in.control, f32[3,64,128]{2,1,0:T(8,128)S(1)} %get-tuple-element.46.places.own, f32[3,64,128]{2,1,0:T(8,128)S(1)} %get-tuple-element.88.burgers, f32[6,48,128]{2,1,0:T(8,128)S(1)} %collective-permute-done.g3, ...), custom_call_target="tpu_custom_call" | custom-call | flops 20000000000 | bytes 1048576 | tf_op jit(solution)/shard_map/near_first/pallas_call | solution.py:639
  39.1 1.0 start.1
  40.2 0.1 collective-permute-start.4
  40.4 5.8 %collective-permute-start.6 = (f32[3,48,128]{2,1,0:T(8,128)S(1)}, f32[3,48,128]{2,1,0:T(8,128)S(1)}, u32[]{:S(2)}, u32[]{:S(2)}) collective-permute-start(f32[3,48,128]{2,1,0:T(8,128)S(1)} %get-tuple-element.58), channel_id=1, source_target_pairs={{0,1},{1,0},{2,3},{3,2},{4,5},{5,4},{6,7},{7,6},{8,9},{9,8},{10,11... | collective-permute-start | bytes 221192 | tf_op jit(solution)/shard_map/ppermute | solution.py:585
  46.2 5.2 %near_early.4 = (bf16[64,8,16,128]{3,2,1,0:T(8,128)(2,1)S(1)}, f32[512,128]{1,0:T(8,128)S(1)}) custom-call(s32[1112]{0:T(1024)S(1)} %get-tuple-element.47.control_in.control, f32[3,64,128]{2,1,0:T(8,128)S(1)} %get-tuple-element.55.own, f32[3,48,128]{2,1,0:T(8,128)S(1)} %collective-permute-done.7.g3, f32[2056,128]{1,0:T(8,128)S(1)} %get-tuple-element.59.burg), custom_call_target="tpu_custom_call" | custom-call | flops 20000000000 | bytes 1048576 | tf_op jit(solution)/shard_map/near_early/pallas_call | solution.py:663
  51.4 6.8 %near_step.3 = (f32[3,64,128]{2,1,0:T(8,128)S(1)}, f32[3,64,128]{2,1,0:T(8,128)S(1)}, f32[3,48,128]{2,1,0:T(8,128)S(1)}, f32[3,48,128]{2,1,0:T(8,128)S(1)}, f32[...) custom-call(s32[1112]{0:T(1024)S(1)} %get-tuple-element.47.control_in.control, ...), custom_call_target="tpu_custom_call" | custom-call | flops 10000000000 | bytes 1048576 | tf_op jit(solution)/shard_map/near_step/pallas_call | solution.py:673
  58.6 4.3 %collective-permute-start.10 = (f32[3,48,128]{2,1,0:T(8,128)S(1)}, f32[3,48,128]{2,1,0:T(8,128)S(1)}, u32[]{:S(2)}, u32[]{:S(2)}) collective-permute-start(f32[3,48,128]{2,1,0:T(8,128)S(1)} %get-tuple-element.67), channel_id=1, source_target_pairs={{0,1},{1,0},{2,3},{3,2},{4,5},{5,4},{6,7},{7,6},{8,9},{9,8},{10,11... | collective-permute-start | bytes 221192 | tf_op jit(solution)/shard_map/ppermute | solution.py:585
  62.9 5.0 %near_early.5 = (bf16[64,8,16,128]{3,2,1,0:T(8,128)(2,1)S(1)}, f32[512,128]{1,0:T(8,128)S(1)}) custom-call(s32[1112]{0:T(1024)S(1)} %get-tuple-element.47.control_in.control, f32[3,64,128]{2,1,0:T(8,128)S(1)} %get-tuple-element.64.own, f32[3,48,128]{2,1,0:T(8,128)S(1)} %collective-permute-done.11.g3, f32[2056,128]{1,0:T(8,128)S(1)} %get-tuple-element.59.burg), custom_call_target="tpu_custom_call" | custom-call | flops 20000000000 | bytes 1048576 | tf_op jit(solution)/shard_map/near_early/pallas_call | solution.py:663
  68.0 6.8 %near_step.4 = (f32[3,64,128]{2,1,0:T(8,128)S(1)}, f32[3,64,128]{2,1,0:T(8,128)S(1)}, f32[3,48,128]{2,1,0:T(8,128)S(1)}, f32[3,48,128]{2,1,0:T(8,128)S(1)}, f32[...) custom-call(s32[1112]{0:T(1024)S(1)} %get-tuple-element.47.control_in.control, ...), custom_call_target="tpu_custom_call" | custom-call | flops 10000000000 | bytes 1048576 | tf_op jit(solution)/shard_map/near_step/pallas_call | solution.py:673
  75.1 4.9 %collective-permute-start.14 = (f32[3,48,128]{2,1,0:T(8,128)S(1)}, f32[3,48,128]{2,1,0:T(8,128)S(1)}, u32[]{:S(2)}, u32[]{:S(2)}) collective-permute-start(f32[3,48,128]{2,1,0:T(8,128)S(1)} %get-tuple-element.75), channel_id=1, source_target_pairs={{0,1},{1,0},{2,3},{3,2},{4,5},{5,4},{6,7},{7,6},{8,9},{9,8},{10,11... | collective-permute-start | bytes 221192 | tf_op jit(solution)/shard_map/ppermute | solution.py:585
  80.0 5.1 %near_early.6 = (bf16[64,8,16,128]{3,2,1,0:T(8,128)(2,1)S(1)}, f32[512,128]{1,0:T(8,128)S(1)}) custom-call(s32[1112]{0:T(1024)S(1)} %get-tuple-element.47.control_in.control, f32[3,64,128]{2,1,0:T(8,128)S(1)} %get-tuple-element.72.own, f32[3,48,128]{2,1,0:T(8,128)S(1)} %collective-permute-done.15.g3, f32[2056,128]{1,0:T(8,128)S(1)} %get-tuple-element.59.burg), custom_call_target="tpu_custom_call" | custom-call | flops 20000000000 | bytes 1048576 | tf_op jit(solution)/shard_map/near_early/pallas_call | solution.py:663
  85.2 7.7 %near_step.5 = (f32[3,8192]{1,0:T(4,128)}, f32[3,64,128]{2,1,0:T(8,128)S(1)}, f32[3,48,128]{2,1,0:T(8,128)S(1)}, f32[3,48,128]{2,1,0:T(8,128)S(1)}, f32[3,48,128...) custom-call(s32[1112]{0:T(1024)S(1)} %get-tuple-element.47.control_in.control, f32[8,128]{1,0:T(8,128)S(1)} %get-tuple-element.54.expansion, ...), custom_call_target="tpu_custom_call" | custom-call | flops 10000000000 | bytes 1048576 | tf_op jit(solution)/shard_map/near_step/pallas_call | solution.py:673
  93.1 4.3 %collective-permute-start.18 = (f32[3,48,128]{2,1,0:T(8,128)S(1)}, f32[3,48,128]{2,1,0:T(8,128)S(1)}, u32[]{:S(2)}, u32[]{:S(2)}) collective-permute-start(f32[3,48,128]{2,1,0:T(8,128)S(1)} %get-tuple-element.84), channel_id=1, source_target_pairs={{0,1},{1,0},{2,3},{3,2},{4,5},{5,4},{6,7},{7,6},{8,9},{9,8},{10,11... | collective-permute-start | bytes 221192 | tf_op jit(solution)/shard_map/ppermute | solution.py:585
  97.5 4.9 %near_early.7 = (bf16[64,8,16,128]{3,2,1,0:T(8,128)(2,1)S(1)}, f32[512,128]{1,0:T(8,128)S(1)}) custom-call(s32[1112]{0:T(1024)S(1)} %get-tuple-element.47.control_in.control, f32[3,64,128]{2,1,0:T(8,128)S(1)} %get-tuple-element.81.own, f32[3,48,128]{2,1,0:T(8,128)S(1)} %collective-permute-done.19.g3, f32[2056,128]{1,0:T(8,128)S(1)} %get-tuple-element.59.burg), custom_call_target="tpu_custom_call" | custom-call | flops 20000000000 | bytes 1048576 | tf_op jit(solution)/shard_map/near_early/pallas_call | solution.py:663
  102.5 7.0 %near_last.1 = f32[3,8192]{1,0:T(4,128)} custom-call(s32[1112]{0:T(1024)S(1)} %get-tuple-element.47.control_in.control, f32[8,128]{1,0:T(8,128)S(1)} %get-tuple-element.54.expansion, f32[3,64,128]{2,1,0:T(8,128)S(1)} %get-tuple-element.81.own, f32[3,48,128]{2,1,0:T(8,128)S(1)} %collective-permute-done.16.g0, f32[3,48,128]{2,1,0:T(8,128)S(1)} %collective-permute-done.17.g2, ...), custom_call_target="tpu_custom_call" | custom-call | flops 10000000000 | bytes 1048576 | tf_op jit(solution)/shard_map/near_last/pallas_call | solution.py:673
  (34 shorter events, 1.1 us)
Async XLA Ops:
  3.7 24.4 %collective-permute-start = (f32[6,48,128]{2,1,0:T(8,128)S(1)}, f32[6,48,128]{2,1,0:T(8,128)S(1)}, u32[]{:S(2)}, u32[]{:S(2)}) collective-permute-start(f32[6,48,128]{2,1,0:T(8,128)S(1)} %get-tuple-element.49), channel_id=1, source_target_pairs={{0,1},{1,0},{2,3},{3,2},{4,5},{5,4},{6,7},{7,6},{8,9},{9,8},{10,11... | collective-permute-start | bytes 442376 | tf_op jit(solution)/shard_map/ppermute | solution.py:585
  4.5 23.6 %collective-permute-start.1 = (f32[6,48,128]{2,1,0:T(8,128)S(1)}, f32[6,48,128]{2,1,0:T(8,128)S(1)}, u32[]{:S(2)}, u32[]{:S(2)}) collective-permute-start(f32[6,48,128]{2,1,0:T(8,128)S(1)} %get-tuple-element.50), channel_id=1, source_target_pairs={{0,32},{1,33},{2,34},{3,35},{4,36},{5,37},{6,38},{7,39},{8,40},{9,... | collective-permute-start | bytes 442376 | tf_op jit(solution)/shard_map/ppermute | solution.py:585
  5.8 22.3 %collective-permute-start.2 = (f32[6,48,128]{2,1,0:T(8,128)S(1)}, f32[6,48,128]{2,1,0:T(8,128)S(1)}, u32[]{:S(2)}, u32[]{:S(2)}) collective-permute-start(f32[6,48,128]{2,1,0:T(8,128)S(1)} %get-tuple-element.51), channel_id=1, source_target_pairs={{0,32},{1,2},{2,1},{3,4},{4,3},{5,6},{6,5},{7,8},{8,7},{9,10},{10,... | collective-permute-start | bytes 442376 | tf_op jit(solution)/shard_map/ppermute | solution.py:585
  8.0 20.2 %collective-permute-start.3 = (f32[6,48,128]{2,1,0:T(8,128)S(1)}, f32[6,48,128]{2,1,0:T(8,128)S(1)}, u32[]{:S(2)}, u32[]{:S(2)}) collective-permute-start(f32[6,48,128]{2,1,0:T(8,128)S(1)} %get-tuple-element.52), channel_id=1, source_target_pairs={{0,1},{1,0},{2,3},{3,2},{4,5},{5,4},{6,7},{7,6},{8,9},{9,8},{10,11... | collective-permute-start | bytes 442376 | tf_op jit(solution)/shard_map/ppermute | solution.py:585
  17.5 21.6 %all-to-all-start = ((f32[256,1,128]{2,1,0:T(1,128)}), f32[256,1,128]{2,1,0:T(1,128)S(1)}, u32[]{:S(2)}, u32[]{:S(2)}) async-start(f32[256,1,128]{2,1,0:T(1,128)} %bitcast.3), calls=%async_computation | async-start | bytes 262144 | tf_op jit(solution)/shard_map/all_to_all | solution.py:637
  28.2 11.0 %copy-start = (f32[8192]{0:T(1024)S(1)}, f32[8192]{0:T(1024)}, u32[]{:S(2)}) copy-start(f32[8192]{0:T(1024)} %param.8) | copy-start | bytes 98308
  40.1 6.1 %collective-permute-start.7 = (f32[3,48,128]{2,1,0:T(8,128)S(1)}, f32[3,48,128]{2,1,0:T(8,128)S(1)}, u32[]{:S(2)}, u32[]{:S(2)}) collective-permute-start(f32[3,48,128]{2,1,0:T(8,128)S(1)} %get-tuple-element.60), channel_id=1, source_target_pairs={{0,1},{1,0},{2,3},{3,2},{4,5},{5,4},{6,7},{7,6},{8,9},{9,8},{10,11... | collective-permute-start | bytes 221192 | tf_op jit(solution)/shard_map/ppermute | solution.py:585
  40.2 11.2 %collective-permute-start.4 = (f32[3,48,128]{2,1,0:T(8,128)S(1)}, f32[3,48,128]{2,1,0:T(8,128)S(1)}, u32[]{:S(2)}, u32[]{:S(2)}) collective-permute-start(f32[3,48,128]{2,1,0:T(8,128)S(1)} %get-tuple-element.56), channel_id=1, source_target_pairs={{0,32},{1,33},{2,34},{3,35},{4,36},{5,37},{6,38},{7,39},{8,40},{9,... | collective-permute-start | bytes 221192 | tf_op jit(solution)/shard_map/ppermute | solution.py:585
  40.3 11.1 %collective-permute-start.5 = (f32[3,48,128]{2,1,0:T(8,128)S(1)}, f32[3,48,128]{2,1,0:T(8,128)S(1)}, u32[]{:S(2)}, u32[]{:S(2)}) collective-permute-start(f32[3,48,128]{2,1,0:T(8,128)S(1)} %get-tuple-element.57), channel_id=1, source_target_pairs={{0,32},{1,2},{2,1},{3,4},{4,3},{5,6},{6,5},{7,8},{8,7},{9,10},{10,... | collective-permute-start | bytes 221192 | tf_op jit(solution)/shard_map/ppermute | solution.py:585
  40.4 11.0 %collective-permute-start.6 = (f32[3,48,128]{2,1,0:T(8,128)S(1)}, f32[3,48,128]{2,1,0:T(8,128)S(1)}, u32[]{:S(2)}, u32[]{:S(2)}) collective-permute-start(f32[3,48,128]{2,1,0:T(8,128)S(1)} %get-tuple-element.58), channel_id=1, source_target_pairs={{0,1},{1,0},{2,3},{3,2},{4,5},{5,4},{6,7},{7,6},{8,9},{9,8},{10,11... | collective-permute-start | bytes 221192 | tf_op jit(solution)/shard_map/ppermute | solution.py:585
  58.3 4.7 %collective-permute-start.11 = (f32[3,48,128]{2,1,0:T(8,128)S(1)}, f32[3,48,128]{2,1,0:T(8,128)S(1)}, u32[]{:S(2)}, u32[]{:S(2)}) collective-permute-start(f32[3,48,128]{2,1,0:T(8,128)S(1)} %get-tuple-element.68), channel_id=1, source_target_pairs={{0,1},{1,0},{2,3},{3,2},{4,5},{5,4},{6,7},{7,6},{8,9},{9,8},{10,11... | collective-permute-start | bytes 221192 | tf_op jit(solution)/shard_map/ppermute | solution.py:585
  58.4 9.6 %collective-permute-start.8 = (f32[3,48,128]{2,1,0:T(8,128)S(1)}, f32[3,48,128]{2,1,0:T(8,128)S(1)}, u32[]{:S(2)}, u32[]{:S(2)}) collective-permute-start(f32[3,48,128]{2,1,0:T(8,128)S(1)} %get-tuple-element.65), channel_id=1, source_target_pairs={{0,32},{1,33},{2,34},{3,35},{4,36},{5,37},{6,38},{7,39},{8,40},{9,... | collective-permute-start | bytes 221192 | tf_op jit(solution)/shard_map/ppermute | solution.py:585
  58.5 9.5 %collective-permute-start.9 = (f32[3,48,128]{2,1,0:T(8,128)S(1)}, f32[3,48,128]{2,1,0:T(8,128)S(1)}, u32[]{:S(2)}, u32[]{:S(2)}) collective-permute-start(f32[3,48,128]{2,1,0:T(8,128)S(1)} %get-tuple-element.66), channel_id=1, source_target_pairs={{0,32},{1,2},{2,1},{3,4},{4,3},{5,6},{6,5},{7,8},{8,7},{9,10},{10,... | collective-permute-start | bytes 221192 | tf_op jit(solution)/shard_map/ppermute | solution.py:585
  58.6 9.4 %collective-permute-start.10 = (f32[3,48,128]{2,1,0:T(8,128)S(1)}, f32[3,48,128]{2,1,0:T(8,128)S(1)}, u32[]{:S(2)}, u32[]{:S(2)}) collective-permute-start(f32[3,48,128]{2,1,0:T(8,128)S(1)} %get-tuple-element.67), channel_id=1, source_target_pairs={{0,1},{1,0},{2,3},{3,2},{4,5},{5,4},{6,7},{7,6},{8,9},{9,8},{10,11... | collective-permute-start | bytes 221192 | tf_op jit(solution)/shard_map/ppermute | solution.py:585
  74.8 5.2 %collective-permute-start.15 = (f32[3,48,128]{2,1,0:T(8,128)S(1)}, f32[3,48,128]{2,1,0:T(8,128)S(1)}, u32[]{:S(2)}, u32[]{:S(2)}) collective-permute-start(f32[3,48,128]{2,1,0:T(8,128)S(1)} %get-tuple-element.76), channel_id=1, source_target_pairs={{0,1},{1,0},{2,3},{3,2},{4,5},{5,4},{6,7},{7,6},{8,9},{9,8},{10,11... | collective-permute-start | bytes 221192 | tf_op jit(solution)/shard_map/ppermute | solution.py:585
  74.9 10.2 %collective-permute-start.12 = (f32[3,48,128]{2,1,0:T(8,128)S(1)}, f32[3,48,128]{2,1,0:T(8,128)S(1)}, u32[]{:S(2)}, u32[]{:S(2)}) collective-permute-start(f32[3,48,128]{2,1,0:T(8,128)S(1)} %get-tuple-element.73), channel_id=1, source_target_pairs={{0,32},{1,33},{2,34},{3,35},{4,36},{5,37},{6,38},{7,39},{8,40},{9,... | collective-permute-start | bytes 221192 | tf_op jit(solution)/shard_map/ppermute | solution.py:585
  75.0 10.1 %collective-permute-start.13 = (f32[3,48,128]{2,1,0:T(8,128)S(1)}, f32[3,48,128]{2,1,0:T(8,128)S(1)}, u32[]{:S(2)}, u32[]{:S(2)}) collective-permute-start(f32[3,48,128]{2,1,0:T(8,128)S(1)} %get-tuple-element.74), channel_id=1, source_target_pairs={{0,32},{1,2},{2,1},{3,4},{4,3},{5,6},{6,5},{7,8},{8,7},{9,10},{10,... | collective-permute-start | bytes 221192 | tf_op jit(solution)/shard_map/ppermute | solution.py:585
  75.1 10.1 %collective-permute-start.14 = (f32[3,48,128]{2,1,0:T(8,128)S(1)}, f32[3,48,128]{2,1,0:T(8,128)S(1)}, u32[]{:S(2)}, u32[]{:S(2)}) collective-permute-start(f32[3,48,128]{2,1,0:T(8,128)S(1)} %get-tuple-element.75), channel_id=1, source_target_pairs={{0,1},{1,0},{2,3},{3,2},{4,5},{5,4},{6,7},{7,6},{8,9},{9,8},{10,11... | collective-permute-start | bytes 221192 | tf_op jit(solution)/shard_map/ppermute | solution.py:585
  92.8 4.6 %collective-permute-start.19 = (f32[3,48,128]{2,1,0:T(8,128)S(1)}, f32[3,48,128]{2,1,0:T(8,128)S(1)}, u32[]{:S(2)}, u32[]{:S(2)}) collective-permute-start(f32[3,48,128]{2,1,0:T(8,128)S(1)} %get-tuple-element.85), channel_id=1, source_target_pairs={{0,1},{1,0},{2,3},{3,2},{4,5},{5,4},{6,7},{7,6},{8,9},{9,8},{10,11... | collective-permute-start | bytes 221192 | tf_op jit(solution)/shard_map/ppermute | solution.py:585
  92.9 9.5 %collective-permute-start.16 = (f32[3,48,128]{2,1,0:T(8,128)S(1)}, f32[3,48,128]{2,1,0:T(8,128)S(1)}, u32[]{:S(2)}, u32[]{:S(2)}) collective-permute-start(f32[3,48,128]{2,1,0:T(8,128)S(1)} %get-tuple-element.82), channel_id=1, source_target_pairs={{0,32},{1,33},{2,34},{3,35},{4,36},{5,37},{6,38},{7,39},{8,40},{9,... | collective-permute-start | bytes 221192 | tf_op jit(solution)/shard_map/ppermute | solution.py:585
  93.0 9.4 %collective-permute-start.17 = (f32[3,48,128]{2,1,0:T(8,128)S(1)}, f32[3,48,128]{2,1,0:T(8,128)S(1)}, u32[]{:S(2)}, u32[]{:S(2)}) collective-permute-start(f32[3,48,128]{2,1,0:T(8,128)S(1)} %get-tuple-element.83), channel_id=1, source_target_pairs={{0,32},{1,2},{2,1},{3,4},{4,3},{5,6},{6,5},{7,8},{8,7},{9,10},{10,... | collective-permute-start | bytes 221192 | tf_op jit(solution)/shard_map/ppermute | solution.py:585
  93.1 9.3 %collective-permute-start.18 = (f32[3,48,128]{2,1,0:T(8,128)S(1)}, f32[3,48,128]{2,1,0:T(8,128)S(1)}, u32[]{:S(2)}, u32[]{:S(2)}) collective-permute-start(f32[3,48,128]{2,1,0:T(8,128)S(1)} %get-tuple-element.84), channel_id=1, source_target_pairs={{0,1},{1,0},{2,3},{3,2},{4,5},{5,4},{6,7},{7,6},{8,9},{9,8},{10,11... | collective-permute-start | bytes 221192 | tf_op jit(solution)/shard_map/ppermute | solution.py:585
